TPU v7x, 256 devices: a whole 4x4x8 slice. The times are simulated.
256 devices in a mesh: dp: 8 (over z), seq: 32 (over y, x, core).
Axes of the slice: x: 4, y: 4, z: 8, core: 2. Of those that a mesh axis runs over, the one named last changes fastest.
Arguments:
- query_tiles: bfloat16 [8, 32, 128, 2048], P('dp', 'seq'), may hold values from -20 to 20
- key_tiles: bfloat16 [8, 32, 128, 2048], P('dp', 'seq'), may hold values from -6 to 6
- value_tiles: bfloat16 [8, 32, 128, 2048], P('dp', 'seq'), may hold values from -6 to 6
- attn_grad: bfloat16 [8, 32, 128, 2048], P('dp', 'seq'), may hold values from -6 to 6
- proj_grad: bfloat16 [8, 32, 128, 3072], P('dp', 'seq'), may hold values from -6 to 6
- neighbour: int32 [8, 32], P('dp'), may hold values from 0 to 31, as said below
Outputs:
- query_grad: bfloat16 [8, 32, 128, 2048], P('dp', 'seq')
- key_grad: bfloat16 [8, 32, 128, 2048], P('dp', 'seq')
- value_grad: bfloat16 [8, 32, 128, 2048], P('dp', 'seq')
- update: float32 [2048, 3072], P('dp', 'seq')
Inputs may be any that keep to these rules, and one draw needn't show every extreme that they name: neighbour[v, t] is t - 1 or t + 1; tile 0 names tile 1, tile 1 names tile 0, tile 32 - 2 names tile 32 - 1 and tile 32 - 1 names tile 32 - 2.
All inputs are finite; a program needn't handle non-finite values.
Results may differ from a plain program's by a relative error of at most 0.024.
Values may be sent and summed in bfloat16 or wider, within the bound.
A program may use at most 128 MiB of HBM per device.

v0:
```python
import jax
import jax.numpy as jnp
from jax import lax
from jax.sharding import PartitionSpec as P

D = 3072
HEAD_DIM = 128
NS_STEPS = 5


coeff_a = 3.4445
coeff_b = -4.775
coeff_c = 2.0315


def padded(cells, sides, width):
    for axis, dim in sides:
        count = lax.axis_size(axis)
        ends = count - 1
        head = lax.slice_in_dim(cells, 0, width, axis=dim)
        tail = lax.slice_in_dim(cells, cells.shape[dim] - width, cells.shape[dim], axis=dim)
        cells = jnp.concatenate(
            [
                lax.ppermute(tail, axis, [(i, (i + 1) % count) for i in range(ends)]),
                cells,
                lax.ppermute(head, axis, [((i + 1) % count, i) for i in range(ends)]),
            ],
            axis=dim,
        )
    return cells


def partner(value, axis, stride):
    mask = 2**stride
    pairs = [(source, source ^ mask) for source in range(lax.axis_size(axis))]
    return lax.ppermute(value, axis, pairs)


def tile_grads(query_rows, key_own, value_own, key_far, value_far, out_grad):
    tile_rows = query_rows.shape[0]
    width = query_rows.shape[1]
    head_count = width // HEAD_DIM
    score_scale = HEAD_DIM ** (-0.5)
    f32 = jnp.float32
    query_h = query_rows.reshape(tile_rows, head_count, HEAD_DIM)
    keys_all = jnp.concatenate([key_own, key_far], 0).reshape(2 * tile_rows, head_count, HEAD_DIM)
    values_all = jnp.concatenate([value_own, value_far], 0).reshape(
        2 * tile_rows, head_count, HEAD_DIM
    )
    grad_h = out_grad.reshape(tile_rows, head_count, HEAD_DIM)
    scores = jnp.einsum("ihd,jhd->hij", query_h, keys_all, preferred_element_type=f32) * score_scale
    row_max = jnp.max(scores, axis=-1, keepdims=True)
    exp_scores = jnp.exp(scores - row_max)
    weights = exp_scores / jnp.sum(exp_scores, axis=-1, keepdims=True)
    weights_b = weights.astype(jnp.bfloat16)
    attended = jnp.einsum("hij,jhd->ihd", weights_b, values_all, preferred_element_type=f32).astype(
        jnp.bfloat16
    )
    row_delta = jnp.sum(grad_h.astype(f32) * attended.astype(f32), axis=-1).T
    dweights = jnp.einsum("ihd,jhd->hij", grad_h, values_all, preferred_element_type=f32)
    dscore_b = (weights * (dweights - row_delta[:, :, None])).astype(jnp.bfloat16)
    query_grad = (
        jnp.einsum("hij,jhd->ihd", dscore_b, keys_all, preferred_element_type=f32) * score_scale
    )
    key_grad = (
        jnp.einsum("hij,ihd->jhd", dscore_b, query_h, preferred_element_type=f32) * score_scale
    )
    value_grad = jnp.einsum("hij,ihd->jhd", weights_b, grad_h, preferred_element_type=f32)
    key_grad = key_grad.reshape(2 * tile_rows, width)
    value_grad = value_grad.reshape(2 * tile_rows, width)
    return (
        query_grad.reshape(tile_rows, width).astype(jnp.bfloat16),
        key_grad[:tile_rows],
        value_grad[:tile_rows],
        key_grad[tile_rows:].astype(jnp.bfloat16),
        value_grad[tile_rows:].astype(jnp.bfloat16),
        attended.reshape(tile_rows, width),
    )


def orthogonalize(grad_rows):
    row_total = grad_rows.shape[0]
    blocks = grad_rows.reshape(row_total // HEAD_DIM, HEAD_DIM, grad_rows.shape[1])
    frob_norm = jnp.sqrt(jnp.sum(blocks * blocks, axis=(1, 2), keepdims=True)) + 1e-07
    iterate = blocks / frob_norm
    best = lax.Precision.HIGHEST
    for turn in range(NS_STEPS):
        gram_matrix = jnp.einsum("hid,hjd->hij", iterate, iterate, precision=best)
        polynomial = coeff_b * gram_matrix + coeff_c * jnp.einsum(
            "hij,hjk->hik", gram_matrix, gram_matrix, precision=best
        )
        iterate = coeff_a * iterate + jnp.einsum(
            "hij,hjd->hid", polynomial, iterate, precision=best
        )
    return (iterate * (0.2 * D**0.5)).reshape(row_total, grad_rows.shape[1])


def split_by_bit(held, bit_value):
    split = held.reshape((2, held.shape[0] // 2) + held.shape[1:])
    kept = lax.dynamic_index_in_dim(split, bit_value, 0, keepdims=False)
    sent = lax.dynamic_index_in_dim(split, 1 - bit_value, 0, keepdims=False)
    return (kept, sent)


def local(query_tiles, key_tiles, value_tiles, attn_grad, proj_grad, neighbour):
    position = lax.axis_index("seq")
    seq_count = lax.axis_size("seq")
    dp_pos = lax.axis_index("dp")
    dp_count = lax.axis_size("dp")
    dp_bits = dp_count.bit_length() - 1
    parity = dp_pos % 2
    targets = neighbour[0]
    tile_ids = lax.iota(jnp.int32, targets.shape[0])
    my_target = jnp.sum(jnp.where(tile_ids == position, targets, 0))
    go_left = my_target < position
    left_sends = jnp.sum(jnp.where((tile_ids == position - 1) & (targets == position), 1, 0)) > 0
    right_sends = jnp.sum(jnp.where((tile_ids == position + 1) & (targets == position), 1, 0)) > 0
    stacked = jnp.concatenate([key_tiles, value_tiles], 0)
    beside_all = padded(stacked, (("seq", 1),), 1)
    remote = jnp.where(go_left, beside_all[:, 0], beside_all[:, 2])
    results = tile_grads(
        query_tiles[0, 0], key_tiles[0, 0], value_tiles[0, 0], remote[0], remote[1], attn_grad[0, 0]
    )
    query_grad, key_own, value_own, key_far, value_far, attended = results
    outgoing = jnp.stack([key_far, value_far])[:, None]
    incoming = padded(outgoing, (("seq", 1),), 1)
    from_left = jnp.where(left_sends, incoming[:, 0].astype(jnp.float32), 0.0)
    from_right = jnp.where(right_sends, incoming[:, 2].astype(jnp.float32), 0.0)
    key_grad = (key_own + from_left[0] + from_right[0]).astype(jnp.bfloat16)
    value_grad = (value_own + from_left[1] + from_right[1]).astype(jnp.bfloat16)
    grad_rows2d = proj_grad[0, 0]
    half = grad_rows2d.shape[1] // 2
    width = attended.shape[1]
    row_block = width // dp_count
    column_width = half // seq_count
    mine_cols = lax.dynamic_slice_in_dim(grad_rows2d, parity * half, half, 1)
    other_cols = lax.dynamic_slice_in_dim(grad_rows2d, (1 - parity) * half, half, 1)
    partner_att, partner_cols = partner((attended, other_cols), "dp", 0)
    pair_att = jnp.concatenate([attended, partner_att], 0)
    pair_grad = jnp.concatenate([mine_cols, partner_cols], 0)
    contract = (((0,), (0,)), ((), ()))
    pair_full = lax.dot_general(pair_att, pair_grad, contract, preferred_element_type=jnp.float32)
    pair_full = lax.optimization_barrier(pair_full.astype(jnp.bfloat16)).astype(jnp.float32)
    held = pair_full.reshape(dp_count // 2, 2, row_block, half)
    for bit in range(dp_bits - 1, 0, -1):
        kept, sent = split_by_bit(held, dp_pos // 2**bit % 2)
        held = kept + partner(sent.astype(jnp.bfloat16), "dp", bit).astype(sent.dtype)
    flat_rows = held[0].transpose(2, 0, 1).reshape(half, 2 * row_block)
    column_sums = lax.psum_scatter(
        flat_rows.astype(jnp.bfloat16), "seq", scatter_dimension=0, tiled=True
    ).astype(jnp.float32)
    pair_blocks = column_sums.reshape(column_width, 2, row_block).transpose(1, 2, 0)
    own_block = lax.dynamic_index_in_dim(pair_blocks, parity, 0, keepdims=False)
    give_block = lax.dynamic_index_in_dim(pair_blocks, 1 - parity, 0, keepdims=False)
    received = partner(give_block.astype(jnp.bfloat16), "dp", 0).astype(give_block.dtype)
    first_half = jnp.where(parity == 0, own_block, received)
    second_half = jnp.where(parity == 0, received, own_block)
    both = jnp.stack([first_half, second_half], 1)
    whole = (
        lax.all_gather(both.astype(jnp.bfloat16), "seq", axis=2, tiled=True)
        .astype(both.dtype)
        .reshape(row_block, 2 * half)
    )
    result = orthogonalize(whole)
    column_count = result.shape[1] // seq_count
    update = lax.dynamic_slice_in_dim(result, position * column_count, column_count, 1)
    return (query_grad[None, None], key_grad[None, None], value_grad[None, None], update)


def solution(mesh):
    placed = (
        P("dp", "seq", None, None),
        P("dp", "seq", None, None),
        P("dp", "seq", None, None),
        P("dp", "seq", None, None),
        P("dp", "seq", None, None),
        P("dp", None),
    )
    return jax.shard_map(
        local,
        mesh=mesh,
        in_specs=placed,
        out_specs=(
            P("dp", "seq", None, None),
            P("dp", "seq", None, None),
            P("dp", "seq", None, None),
            P("dp", "seq"),
        ),
        check_vma=False,
    )
```

profile of v0, /device:TPU:1, one launch (start us, length us, event | category | flops | bytes accessed | tf_op | source)
XLA Modules:
  0.0 490.1 jit_solution(1126802086055863714)
XLA Ops:
  10.9 5.1 %collective-permute-start.1 = (bf16[2,1,128,2048]{2,3,1,0:T(8,128)(2,1)}, bf16[2,1,128,2048]{2,3,1,0:T(8,128)(2,1)S(1)}, u32[]{:S(2)}, u32[]{:S(2)}) collective-permute-start(bf16[2,1,128,2048]{2,3,1,0:T(8,128)(2,1)} %pad_maximum_fusion), channel_id=1, source_target_pairs={{1,0},{2,1},{3,2},{4,3},{5,4},{6,5},{7,6},{8,7},{9,8},{10,9},{11,1... | collective-permute-start | bytes 3145736 | tf_op jit(solution)/shard_map/ppermute | solution.py:26
  24.0 4.1 collective-permute-done.1
  37.9 15.4 %collective-permute-done.5 = bf16[128,1536]{1,0:T(8,128)(2,1)S(1)} collective-permute-done((bf16[128,1536]{1,0:T(8,128)(2,1)S(1)}, bf16[128,1536]{1,0:T(8,128)(2,1)S(1)}, u32[]{:S(2)}, u32[]{:S(2)}) %collective-permute-start.5) | collective-permute-done | bytes 393248 | tf_op jit(solution)/shard_map/ppermute | solution.py:36
  57.9 4.5 copy-done
  64.5 5.2 %collective-permute-start.6 = (bf16[2,2,256,1536]{3,2,1,0:T(8,128)(2,1)}, bf16[2,2,256,1536]{3,2,1,0:T(8,128)(2,1)}, u32[]{:S(2)}, u32[]{:S(2)}) collective-permute-start(bf16[2,2,256,1536]{3,2,1,0:T(8,128)(2,1)} %fusion.2), channel_id=1, source_target_pairs={{0,128},{32,160},{64,192},{96,224},{128,0},{160,32},{192,64},{224,... | collective-permute-start | bytes 9437192 | tf_op jit(solution)/shard_map/ppermute | solution.py:36
  69.6 133.3 %collective-permute-done.6 = bf16[2,2,256,1536]{3,2,1,0:T(8,128)(2,1)} collective-permute-done((bf16[2,2,256,1536]{3,2,1,0:T(8,128)(2,1)}, bf16[2,2,256,1536]{3,2,1,0:T(8,128)(2,1)}, u32[]{:S(2)}, u32[]{:S(2)}) %collective-permute-start.6) | collective-permute-done | bytes 3145760 | tf_op jit(solution)/shard_map/ppermute | solution.py:36
  203.0 5.0 %bitcast_add_fusion = f32[2,2,256,1536]{3,2,1,0:T(8,128)S(1)} fusion(bf16[2,2,256,1536]{3,2,1,0:T(8,128)(2,1)} %collective-permute-done.6, f32[2,2,2,256,1536]{4,3,2,1,0:T(8,128)} %copy-done, s32[]{:T(128)S(6)} %select_n.115), kind=kLoop, calls=%fused_computation.2 | loop fusion | flops 3145728 | bytes 15728644 | tf_op jit(solution)/shard_map/add | solution.py:147
  210.9 65.4 %collective-permute-done.7 = bf16[1,2,256,1536]{3,2,1,0:T(8,128)(2,1)} collective-permute-done((bf16[1,2,256,1536]{3,2,1,0:T(8,128)(2,1)S(1)}, bf16[1,2,256,1536]{3,2,1,0:T(8,128)(2,1)}, u32[]{:S(2)}, u32[]{:S(2)}) %collective-permute-start.7) | collective-permute-done | bytes 1572896 | tf_op jit(solution)/shard_map/ppermute | solution.py:36
  281.0 3.5 fusion.3
  284.4 95.9 %reduce-scatter.2.cloned.1.call-done = bf16[48,512]{1,0:T(8,128)(2,1)} async-done(((bf16[1536,512]{1,0:T(8,128)(2,1)}), bf16[48,512]{1,0:T(8,128)(2,1)}) %reduce-scatter.2.cloned.1.call-update) | async-done | bytes 49168 | tf_op jit(solution)/shard_map/reduce_scatter | solution.py:149
  392.2 4.9 %collective-permute-start.3 = (bf16[2,1,128,2048]{2,3,1,0:T(8,128)(2,1)}, bf16[2,1,128,2048]{2,3,1,0:T(8,128)(2,1)}, u32[]{:S(2)}, u32[]{:S(2)}) collective-permute-start(bf16[2,1,128,2048]{2,3,1,0:T(8,128)(2,1)} %maximum_bitcast_fusion), channel_id=1, source_target_pairs={{1,0},{2,1},{3,2},{4,3},{5,4},{6,5},{7,6},{8,7},{9,8},{10,9},{11,1... | collective-permute-start | bytes 3145736 | tf_op jit(solution)/shard_map/ppermute | solution.py:26
  404.2 7.6 %collective-permute-done.3 = bf16[2,1,128,2048]{2,3,1,0:T(8,128)(2,1)} collective-permute-done((bf16[2,1,128,2048]{2,3,1,0:T(8,128)(2,1)}, bf16[2,1,128,2048]{2,3,1,0:T(8,128)(2,1)}, u32[]{:S(2)}, u32[]{:S(2)}) %collective-permute-start.3) | collective-permute-done | bytes 1048608 | tf_op jit(solution)/shard_map/ppermute | solution.py:26
  416.9 20.1 %all-gather.2.cloned.1.call-done = bf16[256,2,1536]{0,2,1:T(8,128)(2,1)} async-done(((bf16[256,2,48]{0,2,1:T(8,128)(2,1)}), bf16[256,2,1536]{0,2,1:T(8,128)(2,1)}) %all-gather.2.cloned.1.call-update) | async-done | bytes 1572880 | tf_op jit(solution)/shard_map/all_gather | solution.py:160
  438.9 3.1 reshape.183
  442.0 3.6 copy.143
  445.7 6.3 %fusion.26 = f32[2,128,128]{2,1,0:T(8,128)S(1)} fusion(f32[2,128,3072]{2,1,0:T(8,128)} %copy.143, f32[2]{0:T(128)S(1)} %sqrt_add_fusion), kind=kOutput, calls=%fused_computation.63 | convolution fusion | flops 1208745984 | bytes 3276808 | tf_op jit(solution)/shard_map/hid,hjd->hij/dot_general | solution.py:88
  452.2 3.2 convolution_add_fusion.4
  455.4 3.0 fusion.44
  458.7 3.4 convolution_add_fusion.3
  462.1 3.0 fusion.45
  465.3 3.2 convolution_add_fusion.2
  471.8 3.4 convolution_add_fusion.1
  475.2 3.0 fusion.47
  478.5 3.5 fusion.1
  (103 shorter events, 64.5 us)
Async XLA Ops:
  7.2 10.9 %copy-start.16 = (s32[1,32]{1,0:T(1,128)S(1)}, s32[1,32]{1,0:T(1,128)}, u32[]{:S(2)}) copy-start(s32[1,32]{1,0:T(1,128)} %param.11) | copy-start | bytes 388
  7.2 373.2 %reduce-scatter.2.cloned.1.call-start = ((), (), s32[]{:S(2)}) async-start(), calls=%async_computation.1 | async-start | bytes 1622016 | tf_op jit(solution)/shard_map/reduce_scatter | solution.py:149
  10.9 17.2 %collective-permute-start.1 = (bf16[2,1,128,2048]{2,3,1,0:T(8,128)(2,1)}, bf16[2,1,128,2048]{2,3,1,0:T(8,128)(2,1)S(1)}, u32[]{:S(2)}, u32[]{:S(2)}) collective-permute-start(bf16[2,1,128,2048]{2,3,1,0:T(8,128)(2,1)} %pad_maximum_fusion), channel_id=1, source_target_pairs={{1,0},{2,1},{3,2},{4,3},{5,4},{6,5},{7,6},{8,7},{9,8},{10,9},{11,1... | collective-permute-start | bytes 3145736 | tf_op jit(solution)/shard_map/ppermute | solution.py:26
  16.1 14.0 %collective-permute-start = (bf16[2,1,128,2048]{2,3,1,0:T(8,128)(2,1)}, bf16[2,1,128,2048]{2,3,1,0:T(8,128)(2,1)}, u32[]{:S(2)}, u32[]{:S(2)}) collective-permute-start(bf16[2,1,128,2048]{2,3,1,0:T(8,128)(2,1)} %pad_maximum_fusion), channel_id=1, source_target_pairs={{0,1},{1,2},{2,3},{3,4},{4,5},{5,6},{6,7},{7,8},{8,9},{9,10},{10,1... | collective-permute-start | bytes 3145736 | tf_op jit(solution)/shard_map/ppermute | solution.py:24
  19.7 13.1 %copy-start.4 = (bf16[128,16,128]{2,0,1:T(8,128)(2,1)}, bf16[128,16,128]{2,0,1:T(8,128)(2,1)S(1)}, u32[]{:S(2)}) copy-start(bf16[128,16,128]{2,0,1:T(8,128)(2,1)S(1)} %copy.110) | copy-start | bytes 1572868
  31.8 3.0 copy-start.6
  32.8 2.1 copy-start.15
  34.8 2.5 copy-start.11
  36.3 17.0 %collective-permute-start.4 = (bf16[128,2048]{0,1:T(8,128)(2,1)}, bf16[128,2048]{0,1:T(8,128)(2,1)S(1)}, u32[]{:S(2)}, u32[]{:S(2)}) collective-permute-start(bf16[128,2048]{0,1:T(8,128)(2,1)} %bitcast.19), channel_id=1, source_target_pairs={{0,32},{32,0},{64,96},{96,64},{128,160},{160,128},{192,224},{224,1... | collective-permute-start | bytes 1572872 | tf_op jit(solution)/shard_map/ppermute | solution.py:36
  37.4 15.9 %collective-permute-start.5 = (bf16[128,1536]{1,0:T(8,128)(2,1)S(1)}, bf16[128,1536]{1,0:T(8,128)(2,1)S(1)}, u32[]{:S(2)}, u32[]{:S(2)}) collective-permute-start(bf16[128,1536]{1,0:T(8,128)(2,1)S(1)} %get-tuple-element.32), channel_id=1, source_target_pairs={{0,32},{32,0},{64,96},{96,64},{128,160},{160,128},{192,224},{224,1... | collective-permute-start | bytes 1179656 | tf_op jit(solution)/shard_map/ppermute | solution.py:36
  57.9 4.5 copy-start
  64.5 138.5 %collective-permute-start.6 = (bf16[2,2,256,1536]{3,2,1,0:T(8,128)(2,1)}, bf16[2,2,256,1536]{3,2,1,0:T(8,128)(2,1)}, u32[]{:S(2)}, u32[]{:S(2)}) collective-permute-start(bf16[2,2,256,1536]{3,2,1,0:T(8,128)(2,1)} %fusion.2), channel_id=1, source_target_pairs={{0,128},{32,160},{64,192},{96,224},{128,0},{160,32},{192,64},{224,... | collective-permute-start | bytes 9437192 | tf_op jit(solution)/shard_map/ppermute | solution.py:36
  208.0 2.7 copy-start.1
  210.8 65.6 %collective-permute-start.7 = (bf16[1,2,256,1536]{3,2,1,0:T(8,128)(2,1)S(1)}, bf16[1,2,256,1536]{3,2,1,0:T(8,128)(2,1)}, u32[]{:S(2)}, u32[]{:S(2)}) collective-permute-start(bf16[1,2,256,1536]{3,2,1,0:T(8,128)(2,1)S(1)} %dynamic-slice_convert_fusion.1), channel_id=1, source_target_pairs={{0,64},{32,96},{64,0},{96,32},{128,192},{160,224},{192,128},{224,1... | collective-permute-start | bytes 4718600 | tf_op jit(solution)/shard_map/ppermute | solution.py:36
  280.9 156.0 %all-gather.2.cloned.1.call-start = ((), (), s32[]{:S(2)}) async-start(), calls=%async_computation.2 | async-start | bytes 1622016 | tf_op jit(solution)/shard_map/all_gather | solution.py:160
  281.0 102.2 %copy-start.9 = (f32[16,128,256]{1,2,0:T(8,128)S(1)}, f32[16,128,256]{1,2,0:T(8,128)}, u32[]{:S(2)}) copy-start(f32[16,128,256]{1,2,0:T(8,128)} %copy-done.8) | copy-start | bytes 6291460
  381.3 3.7 collective-permute-start.8
  387.3 13.8 %copy-start.2 = (f32[256,16,128]{2,0,1:T(8,128)}, f32[256,16,128]{2,0,1:T(8,128)S(1)}, u32[]{:S(2)}) copy-start(f32[256,16,128]{2,0,1:T(8,128)S(1)} %multiply_bitcast_fusion) | copy-start | bytes 6291460
  389.9 11.2 %copy-start.5 = (bf16[128,16,128]{2,0,1:T(8,128)(2,1)S(1)}, bf16[128,16,128]{2,0,1:T(8,128)(2,1)}, u32[]{:S(2)}) copy-start(bf16[128,16,128]{2,0,1:T(8,128)(2,1)} %copy-done.4) | copy-start | bytes 1572868
  389.9 11.2 %copy-start.7 = (bf16[128,16,128]{2,0,1:T(8,128)(2,1)S(1)}, bf16[128,16,128]{2,0,1:T(8,128)(2,1)}, u32[]{:S(2)}) copy-start(bf16[128,16,128]{2,0,1:T(8,128)(2,1)} %copy-done.6) | copy-start | bytes 1572868
  392.2 19.6 %collective-permute-start.3 = (bf16[2,1,128,2048]{2,3,1,0:T(8,128)(2,1)}, bf16[2,1,128,2048]{2,3,1,0:T(8,128)(2,1)}, u32[]{:S(2)}, u32[]{:S(2)}) collective-permute-start(bf16[2,1,128,2048]{2,3,1,0:T(8,128)(2,1)} %maximum_bitcast_fusion), channel_id=1, source_target_pairs={{1,0},{2,1},{3,2},{4,3},{5,4},{6,5},{7,6},{8,7},{9,8},{10,9},{11,1... | collective-permute-start | bytes 3145736 | tf_op jit(solution)/shard_map/ppermute | solution.py:26
  397.1 16.0 %collective-permute-start.2 = (bf16[2,1,128,2048]{2,3,1,0:T(8,128)(2,1)}, bf16[2,1,128,2048]{2,3,1,0:T(8,128)(2,1)}, u32[]{:S(2)}, u32[]{:S(2)}) collective-permute-start(bf16[2,1,128,2048]{2,3,1,0:T(8,128)(2,1)} %maximum_bitcast_fusion), channel_id=1, source_target_pairs={{0,1},{1,2},{2,3},{3,4},{4,5},{5,6},{6,7},{7,8},{8,9},{9,10},{10,1... | collective-permute-start | bytes 3145736 | tf_op jit(solution)/shard_map/ppermute | solution.py:24
  404.2 10.3 %slice-start.1 = ((f32[256,16,128]{0,2,1:T(8,128)}), f32[128,16,128]{0,2,1:T(8,128)S(1)}, s32[]{:S(2)}) async-start(f32[256,16,128]{0,2,1:T(8,128)} %convolution_bitcast_fusion), calls=%async_computation.4 | async-start | bytes 2097152 | tf_op jit(solution)/shard_map/slice | solution.py:74
  445.6 6.6 %copy-start.3 = (f32[2,128,3072]{2,1,0:T(8,128)S(1)}, f32[2,128,3072]{2,1,0:T(8,128)}, u32[]{:S(2)}) copy-start(f32[2,128,3072]{2,1,0:T(8,128)} %copy.143) | copy-start | bytes 9437188
  (6 other events, 10.0 us)
Sparse Core Ops, SparseCore 0:
  281.0 99.2 reduce-scatter.1
  385.7 51.1 all-gather.1
where the time goes:
time: 499 us; the launch traced here: 490 us
  waiting for transfers between devices  344 us (69%)
  matrix products  48.3 us (10%)
  local copies, waits for them, and re-layouts  35.5 us (7%)
  starting transfers between devices  23.5 us (5%)
  other arithmetic  22.1 us (4%)
  between operations  17 us (3%)
    ppermute x5, waiting for transfers between devices, partner(): return lax.ppermute(value, axis, pairs)  214 us
    reduce_scatter x1, waiting for transfers between devices, local(): lax.psum_scatter(flat_rows.astype(jnp.bfloat16), 'seq', scatter_dimension...  95.9 us
    all_gather x1, waiting for transfers between devices, local(): lax.all_gather(both.astype(jnp.bfloat16), 'seq', axis=2, tiled=True)  20.1 us
    dot_general x5, matrix products, orthogonalize(): gram_matrix = jnp.einsum('hid,hjd->hij', iterate, iterate, precision=best)  18.2 us
    unnamed x42, local copies, waits for them, and re-layouts  16.9 us
    dot_general x5, matrix products, orthogonalize(): jnp.einsum('hij,hjd->hid', polynomial, iterate, precision=best)  16.7 us
    ppermute x2, waiting for transfers between devices, padded(): lax.ppermute(head, axis, [((i + 1) % count, i) for i in range(ends)])  11.6 us
    ppermute x2, starting transfers between devices, padded(): lax.ppermute(head, axis, [((i + 1) % count, i) for i in range(ends)])  10.1 us
  transfers between devices with their start and end apart: 11, of which 8 were waited for; matrix products, arithmetic and copies ran while one was open for 5% of the time, Pallas kernels for 0%

commit v1 on v0

v1 whole, which is shorter than its diff:
```python
import functools

import jax
import jax.numpy as jnp
from jax import lax
from jax.experimental import pallas as pl
from jax.experimental.pallas import tpu as pltpu
from jax.sharding import PartitionSpec as P

D = 3072
HEAD_DIM = 128
NS_STEPS = 5
MESH = pl.DeviceIdType.MESH
F32 = jnp.float32
BF16 = jnp.bfloat16
BEST = lax.Precision.HIGHEST

coeff_a = 3.4445
coeff_b = -4.775
coeff_c = 2.0315

NT = (((1,), (1,)), ((), ()))
NN = (((1,), (0,)), ((), ()))
TN = (((0,), (0,)), ((), ()))


def mm(a, b, dims):
    return lax.dot_general(a, b, dims, preferred_element_type=F32)


def mmh(a, b, dims=NN):
    return lax.dot_general(a, b, dims, precision=BEST, preferred_element_type=F32)


def head_grads(q, kk, vv, do):
    score_scale = HEAD_DIM ** (-0.5)
    scores = mm(q, kk, NT) * score_scale
    row_max = jnp.max(scores, axis=1, keepdims=True)
    exp_scores = jnp.exp(scores - row_max)
    weights = exp_scores / jnp.sum(exp_scores, axis=1, keepdims=True)
    weights_b = weights.astype(BF16)
    attended = mm(weights_b, vv, NN).astype(BF16)
    delta = jnp.sum(do.astype(F32) * attended.astype(F32), axis=1, keepdims=True)
    dweights = mm(do, vv, NT)
    dscore_b = (weights * (dweights - delta)).astype(BF16)
    dq = (mm(dscore_b, kk, NN) * score_scale).astype(BF16)
    dk = mm(dscore_b, q, TN) * score_scale
    dv = mm(weights_b, do, TN)
    return dq, dk, dv, attended


def kernel(
    geo,
    flags,
    q_hbm, k_hbm, v_hbm, do_hbm, proj_hbm,
    dq_ref, dk_ref, dv_ref, upd_ref,
    q_v, k_v, v_v, do_v,
    halo, far_out, far_in, own_k, own_v,
    proj_all, proj_t, att, part, rx, xsum, rz,
    g_part, g_in, g_full,
    in_sem,
    halo_s, halo_r, far_s, far_r,
    proj_s, proj_r, fwd_s, fwd_r,
    att_s, att_r, x_s, x_r, z_s, z_r,
    g1_s, g1_r, g2_s, g2_r,
):
    nz, ny, nx = geo
    seq = ny * nx * 2
    half_count = nz // 2
    tile = q_v.shape[0]
    cb = 2 * HEAD_DIM
    qcols = proj_all.shape[2]
    xcols = qcols // nx
    ccols = xcols // 2
    z = lax.axis_index("dp")
    s = lax.axis_index("seq")
    c = lax.rem(s, 2)
    x = lax.rem(s // 2, nx)
    y = s // (2 * nx)
    right = (z, lax.rem(s + 1, seq))
    left = (z, lax.rem(s + seq - 1, seq))

    def at(yy, xx, cc):
        return (z, (yy * nx + xx) * 2 + cc)

    def block_of(core, i, e):
        half = lax.rem(core + e, 2)
        return half * half_count + lax.rem(z + i, half_count)

    def lanes(block):
        return pl.ds(pl.multiple_of(block * cb, cb), cb)

    def remote(src, dst, ss, rs, dev):
        return pltpu.make_async_remote_copy(
            src_ref=src, dst_ref=dst, send_sem=ss, recv_sem=rs,
            device_id=dev, device_id_type=MESH,
        )

    own_cols = pl.ds(pl.multiple_of(y * qcols, qcols), qcols)
    loads = [
        pltpu.make_async_copy(q_hbm, q_v, in_sem.at[0]),
        pltpu.make_async_copy(k_hbm, k_v, in_sem.at[1]),
        pltpu.make_async_copy(v_hbm, v_v, in_sem.at[2]),
        pltpu.make_async_copy(do_hbm, do_v, in_sem.at[3]),
        pltpu.make_async_copy(proj_hbm.at[:, own_cols], proj_all.at[0], in_sem.at[4]),
    ]
    for load in loads:
        load.start()

    barrier = pltpu.get_barrier_semaphore()

    def greet_seq(r, carry):
        pl.semaphore_signal(
            barrier, inc=1, device_id=(z, lax.rem(s + r, seq)), device_id_type=MESH
        )
        return carry

    def greet_z(r, carry):
        for e in range(2):
            pl.semaphore_signal(
                barrier, inc=1,
                device_id=(lax.rem(z + r, nz), s - c + e), device_id_type=MESH,
            )
        return carry

    lax.fori_loop(1, seq, greet_seq, 0)
    lax.fori_loop(1, nz, greet_z, 0)
    pl.semaphore_wait(barrier, seq - 1 + 2 * (nz - 1))

    def halo_copy(i, e, kv, way):
        t = 2 * i + e
        src = (k_hbm, v_hbm)[kv].at[:, lanes(block_of(1 - c, i, e))]
        return remote(
            src, halo.at[way, kv, t], halo_s.at[way, kv, t], halo_r.at[way, kv, t],
            (right, left)[way],
        )

    def start_halo(i, carry):
        for e in range(2):
            for kv in range(2):
                for way in range(2):
                    halo_copy(i, e, kv, way).start()
        return carry

    lax.fori_loop(0, half_count, start_halo, 0)

    def proj_copy(d):
        yy = lax.rem(y + d, ny)
        cols = pl.ds(pl.multiple_of(yy * qcols, qcols), qcols)
        return remote(
            proj_hbm.at[:, cols], proj_all.at[2 * d], proj_s.at[d], proj_r.at[d],
            at(yy, x, c),
        )

    def fwd_copy(d):
        src = proj_hbm.at[:, own_cols] if d == 0 else proj_all.at[2 * d]
        return remote(
            src, proj_all.at[2 * d + 1], fwd_s.at[d], fwd_r.at[d], at(y, x, 1 - c)
        )

    for d in range(1, ny):
        proj_copy(d).start()
    fwd_copy(0).start()
    for load in loads:
        load.wait()

    go_left = flags[0]
    go_right = flags[1]
    left_sends = flags[2]
    right_sends = flags[3]

    def att_copy(i, e, d):
        slot = 2 * d + e
        place = pl.ds(slot * tile, tile)
        dst = att.at[i, place]
        return remote(
            far_out.at[2, 2 * i + e], dst, att_s.at[i, slot], att_r.at[i, slot],
            at(lax.rem(y + d, ny), x, lax.rem(c + e, 2)),
        )

    def far_copy(i, e, kv, way):
        t = 2 * i + e
        return remote(
            far_out.at[kv, t], far_in.at[way, kv, t], far_s.at[way, kv, t],
            far_r.at[way, kv, t], (right, left)[way],
        )

    def attend(i, carry):
        for e in range(2):
            t = 2 * i + e
            block = block_of(c, i, e)
            for kv in range(2):
                for way in range(2):
                    halo_copy(i, e, kv, way).wait_recv()
            for h in range(2):
                inside = pl.ds(h * HEAD_DIM, HEAD_DIM)
                cols = pl.ds(
                    pl.multiple_of(block * cb + h * HEAD_DIM, HEAD_DIM), HEAD_DIM
                )

                def beside(kv):
                    from_left = halo[0, kv, t, :, inside].astype(F32) * go_left
                    from_right = halo[1, kv, t, :, inside].astype(F32) * go_right
                    return (from_left + from_right).astype(BF16)

                q = q_v[:, cols]
                do = do_v[:, cols]
                kk = jnp.concatenate([k_v[:, cols], beside(0)], 0)
                vv = jnp.concatenate([v_v[:, cols], beside(1)], 0)
                dq, dk, dv, attended = head_grads(q, kk, vv, do)
                dq_ref[:, cols] = dq
                own_k[:, cols] = dk[:tile]
                own_v[:, cols] = dv[:tile]
                far_out[0, t, :, inside] = dk[tile:].astype(BF16)
                far_out[1, t, :, inside] = dv[tile:].astype(BF16)
                far_out[2, t, :, inside] = attended
            if e == 0:
                att[i, pl.ds(0, tile)] = far_out[2, t]
            for d in range(e == 0, ny):
                att_copy(i, e, d).start()
            for kv in range(2):
                for way in range(2):
                    far_copy(i, e, kv, way).start()
        return carry

    lax.fori_loop(0, half_count, attend, 0)

    for d in range(1, ny):
        proj_copy(d).wait_recv()
        fwd_copy(d).start()

    def turn(slot):
        proj_t[:, slot * tile : (slot + 1) * tile] = proj_all[slot].T

    for d in range(ny):
        turn(2 * d)
    for d in range(ny):
        fwd_copy(d).wait_recv()
        turn(2 * d + 1)

    def x_copy(i, d):
        xx = lax.rem(x + d, nx)
        rows = pl.ds(pl.multiple_of(xx * xcols, xcols), xcols)
        return remote(
            part.at[i, rows], rx.at[i, d], x_s.at[i, d], x_r.at[i, d], at(y, xx, c)
        )

    def z_copy(i, e):
        zz = block_of(c, i, 0)
        cc = lax.rem(c + e, 2)
        rows = pl.ds(pl.multiple_of(cc * ccols, ccols), ccols)
        slot = lax.rem(zz - z + nz, nz)
        return remote(
            xsum.at[i, rows], rz.at[slot], z_s.at[i, e], z_r.at[slot],
            (zz, s - c + cc),
        )

    def product(i):
        for d in range(ny):
            for e in range(2):
                if d + e > 0:
                    att_copy(i, e, d).wait_recv()
        part[i] = mm(proj_t[...], att[i], NN).astype(BF16)
        for d in range(1, nx):
            x_copy(i, d).start()

    def add_x(i):
        mine = pl.ds(pl.multiple_of(x * xcols, xcols), xcols)
        total = part[i, mine].astype(F32)
        for d in range(1, nx):
            x_copy(i, d).wait_recv()
            total = total + rx[i, d].astype(F32)
        xsum[i] = total.astype(BF16)
        zz = block_of(c, i, 0)

        @pl.when(zz == z)
        def _():
            rz[0] = xsum[i, pl.ds(pl.multiple_of(c * ccols, ccols), ccols)]

        @pl.when(zz != z)
        def _():
            z_copy(i, 0).start()

        z_copy(i, 1).start()

    def step(i, carry):
        @pl.when(i < half_count)
        def _():
            product(i)

        @pl.when(i > 0)
        def _():
            add_x(i - 1)

        return carry

    lax.fori_loop(0, half_count + 1, step, 0)

    def gather_far(i, carry):
        for e in range(2):
            t = 2 * i + e
            cols = lanes(block_of(1 - c, i, e))
            for kv in range(2):
                for way in range(2):
                    far_copy(i, e, kv, way).wait_recv()
                own = (own_k, own_v)[kv][:, cols]
                out = (dk_ref, dv_ref)[kv]
                out[:, cols] = (
                    own
                    + far_in[0, kv, t].astype(F32) * left_sends
                    + far_in[1, kv, t].astype(F32) * right_sends
                ).astype(BF16)
        return carry

    lax.fori_loop(0, half_count, gather_far, 0)

    def rz_copy(slot):
        return remote(rz.at[slot], rz.at[slot], z_s.at[0, 1], z_r.at[slot], right)

    @pl.when(c != z // half_count)
    def _():
        rz_copy(0).wait_recv()

    grad = rz[0].astype(F32)
    for slot in range(1, nz):
        rz_copy(slot).wait_recv()
        grad = grad + rz[slot].astype(F32)

    piece = cb // seq
    for h in range(2):
        part_h = grad[:, h * HEAD_DIM : (h + 1) * HEAD_DIM]
        g_part[h * HEAD_DIM : (h + 1) * HEAD_DIM] = mmh(part_h, part_h, TN)

    def rows_of(index):
        return pl.ds(pl.multiple_of(index * piece, piece), piece)

    def g1_copy(r):
        other = lax.rem(s + r, seq)
        return remote(
            g_part.at[rows_of(other)], g_in.at[r], g1_s.at[r], g1_r.at[r], (z, other)
        )

    def g2_copy(r):
        other = lax.rem(s + r, seq)
        return remote(
            g_full.at[rows_of(s)], g_full.at[rows_of(s)], g2_s.at[r], g2_r.at[r],
            (z, other),
        )

    def g2_from(r):
        source = rows_of(lax.rem(s + seq - r, seq))
        return remote(
            g_full.at[source], g_full.at[source], g2_s.at[r], g2_r.at[r], right
        )

    def loop(body):
        def run(r, carry):
            body(r)
            return carry

        lax.fori_loop(1, seq, run, 0)

    loop(lambda r: g1_copy(r).start())

    def add_g(r, total):
        g1_copy(r).wait_recv()
        return total + g_in[r]

    g_full[rows_of(s)] = lax.fori_loop(1, seq, add_g, g_part[rows_of(s)])
    loop(lambda r: g2_copy(r).start())
    loop(lambda r: g2_from(r).wait_recv())

    row_id = lax.broadcasted_iota(jnp.int32, (HEAD_DIM, HEAD_DIM), 0)
    col_id = lax.broadcasted_iota(jnp.int32, (HEAD_DIM, HEAD_DIM), 1)
    eye = jnp.where(row_id == col_id, 1.0, 0.0).astype(F32)
    gram, norm, whole = [], [], [None, None]
    for h in range(2):
        g = g_full[h * HEAD_DIM : (h + 1) * HEAD_DIM]
        trace = jnp.sum(jnp.sum(g * eye, axis=1, keepdims=True), axis=0, keepdims=True)
        n = jnp.sqrt(trace) + 1e-07
        norm.append(n)
        gram.append(g / n / n)
    for turn_id in range(NS_STEPS):
        square = [mmh(g, g) for g in gram]
        poly = [
            coeff_a * eye + coeff_b * g + coeff_c * g2 for g, g2 in zip(gram, square)
        ]
        if turn_id < NS_STEPS - 1:
            half_way = [mmh(p, g) for p, g in zip(poly, gram)]
        whole = [p if w is None else mmh(p, w) for p, w in zip(poly, whole)]
        if turn_id < NS_STEPS - 1:
            gram = [mmh(t, p) for t, p in zip(half_way, poly)]
    for h in range(2):
        part_h = grad[:, h * HEAD_DIM : (h + 1) * HEAD_DIM]
        result = mmh(whole[h], part_h / norm[h], NT)
        upd_ref[h * HEAD_DIM : (h + 1) * HEAD_DIM] = result * (0.2 * D**0.5)

    def drain(i, carry):
        for e in range(2):
            for kv in range(2):
                for way in range(2):
                    halo_copy(i, e, kv, way).wait_send()
                    far_copy(i, e, kv, way).wait_send()
            for d in range(e == 0, ny):
                att_copy(i, e, d).wait_send()
        for d in range(1, nx):
            x_copy(i, d).wait_send()

        @pl.when(block_of(c, i, 0) != z)
        def _():
            z_copy(i, 0).wait_send()

        z_copy(i, 1).wait_send()
        return carry

    lax.fori_loop(0, half_count, drain, 0)
    for d in range(ny):
        if d > 0:
            proj_copy(d).wait_send()
        fwd_copy(d).wait_send()
    loop(lambda r: g1_copy(r).wait_send())
    loop(lambda r: g2_copy(r).wait_send())


def local(geo, query_tiles, key_tiles, value_tiles, attn_grad, proj_grad, neighbour):
    nz, ny, nx = geo
    seq = ny * nx * 2
    hc = nz // 2
    position = lax.axis_index("seq")
    tile, width = query_tiles.shape[2:]
    depth = proj_grad.shape[3]
    qcols = depth // ny
    xcols = qcols // nx
    cb = 2 * HEAD_DIM
    group = ny * 2
    targets = neighbour[0]
    tile_ids = lax.iota(jnp.int32, targets.shape[0])
    go_left = jnp.any((tile_ids == position) & (targets < position))
    left_sends = jnp.any((tile_ids == position - 1) & (targets == position))
    right_sends = jnp.any((tile_ids == position + 1) & (targets == position))
    flags = jnp.stack([go_left, ~go_left, left_sends, right_sends]).astype(F32)
    vm = pl.BlockSpec(memory_space=pltpu.VMEM)
    anyspec = pl.BlockSpec(memory_space=pl.ANY)
    rows = jax.ShapeDtypeStruct((tile, width), BF16)
    dma = pltpu.SemaphoreType.DMA
    out = pl.pallas_call(
        functools.partial(kernel, geo),
        out_shape=(rows, rows, rows, jax.ShapeDtypeStruct((cb, depth // seq), F32)),
        in_specs=[pl.BlockSpec(memory_space=pltpu.SMEM)] + [anyspec] * 5,
        out_specs=(vm, vm, vm, vm),
        scratch_shapes=[pltpu.VMEM((tile, width), BF16)] * 4
        + [
            pltpu.VMEM((2, 2, 2 * hc, tile, cb), BF16),
            pltpu.VMEM((3, 2 * hc, tile, cb), BF16),
            pltpu.VMEM((2, 2, 2 * hc, tile, cb), BF16),
            pltpu.VMEM((tile, width), F32),
            pltpu.VMEM((tile, width), F32),
            pltpu.VMEM((group, tile, qcols), BF16),
            pltpu.VMEM((qcols, group * tile), BF16),
            pltpu.VMEM((hc, group * tile, cb), BF16),
            pltpu.VMEM((hc, qcols, cb), BF16),
            pltpu.VMEM((hc, nx, xcols, cb), BF16),
            pltpu.VMEM((hc, xcols, cb), BF16),
            pltpu.VMEM((nz, xcols // 2, cb), BF16),
            pltpu.VMEM((cb, HEAD_DIM), F32),
            pltpu.VMEM((seq, cb // seq, HEAD_DIM), F32),
            pltpu.VMEM((cb, HEAD_DIM), F32),
            dma((5,)),
            dma((2, 2, 2 * hc)), dma((2, 2, 2 * hc)),
            dma((2, 2, 2 * hc)), dma((2, 2, 2 * hc)),
            dma((ny,)), dma((ny,)), dma((ny,)), dma((ny,)),
            dma((hc, group)), dma((hc, group)),
            dma((hc, nx)), dma((hc, nx)),
            dma((hc, 2)), dma((nz,)),
            dma((seq,)), dma((seq,)), dma((seq,)), dma((seq,)),
        ],
        compiler_params=pltpu.CompilerParams(
            collective_id=0, has_side_effects=True, vmem_limit_bytes=48 * 2**20
        ),
    )(
        flags, query_tiles[0, 0], key_tiles[0, 0], value_tiles[0, 0], attn_grad[0, 0],
        proj_grad[0, 0],
    )
    return out[0][None, None], out[1][None, None], out[2][None, None], out[3]


def solution(mesh):
    nz, seq = mesh.shape["dp"], mesh.shape["seq"]
    nx = 4 if seq == 32 else 2
    geo = (nz, seq // (2 * nx), nx)
    tiled = P("dp", "seq", None, None)
    return jax.shard_map(
        functools.partial(local, geo),
        mesh=mesh,
        in_specs=(tiled, tiled, tiled, tiled, tiled, P("dp", None)),
        out_specs=(tiled, tiled, tiled, P("dp", "seq")),
        check_vma=False,
    )
```

time: 499 us -> 112 us (0.22); the launches traced: 490 us -> 111 us
  waiting for transfers between devices: 344 us -> 0 us
  Pallas kernels: 0 us -> 98.4 us
  matrix products: 48.3 us -> 0 us
  local copies, waits for them, and re-layouts: 35.5 us -> 9.06 us
  starting transfers between devices: 23.5 us -> 0 us
  other arithmetic: 22.1 us -> 2.69 us
  between operations: 17 us -> 1.31 us
    ppermute x9 -> x0, waiting for transfers between devices: 228 us -> none  [the longest x5 214 us: partner(): return lax.ppermute(value, axis, pairs)]
    pallas_call x0 -> x1, Pallas kernels: none -> 98.4 us  [local(): pl.pallas_call(functools.partial(kernel, geo), out_shape=(rows, rows, row...]
    reduce_scatter x1 -> x0, waiting for transfers between devices: 95.9 us -> none  [local(): lax.psum_scatter(flat_rows.astype(jnp.bfloat16), 'seq', scatter_dimension...]
    dot_general x22 -> x0, matrix products: 48.3 us -> none  [the longest x5 18.2 us: orthogonalize(): gram_matrix = jnp.einsum('hid,hjd->hij', iterate, iterate, precision=best)]
    ppermute x9 -> x0, starting transfers between devices: 23.4 us -> none  [the longest x2 10.1 us: padded(): lax.ppermute(head, axis, [((i + 1) % count, i) for i in range(ends)])]
    all_gather x1 -> x0, waiting for transfers between devices: 20.1 us -> none  [local(): lax.all_gather(both.astype(jnp.bfloat16), 'seq', axis=2, tiled=True)]
    another operation x3 -> x0, local copies, waits for them, and re-layouts: 8.05 us -> none  [the longest x2 6.74 us: orthogonalize(): grad_rows.reshape(row_total // HEAD_DIM, HEAD_DIM, grad_rows.shape[1])]
    unnamed x42 -> x16, local copies, waits for them, and re-layouts: 16.9 us -> 9.06 us
  transfers between devices with their start and end apart: 11 -> 0, of which waited for: 8 -> 0; matrix products, arithmetic and copies ran while one was open for 5% -> 0% of each run, Pallas kernels for 0% -> 0%
where the time goes in v1:
time: 112 us; the launch traced here: 111 us
  Pallas kernels  98.4 us (88%)
  local copies, waits for them, and re-layouts  9.06 us (8%)
  other arithmetic  2.69 us (2%)
  between operations  1.31 us (1%)
    pallas_call x1, Pallas kernels, local(): pl.pallas_call(functools.partial(kernel, geo), out_shape=(rows, rows, row...  98.4 us
    unnamed x16, local copies, waits for them, and re-layouts  9.06 us

profile of v1, /device:TPU:1, one launch (start us, length us, event | category | flops | bytes accessed | tf_op | source)
XLA Modules:
  0.0 111.4 jit_solution(13289087067358002347)
XLA Ops:
  0.6 0.0 copy-start.5
  0.6 0.6 copy-done.5
  1.3 0.7 fusion.2
  2.6 2.0 %add_convert_fusion.flags = f32[4]{0:T(128)S(1)} fusion(pred[1]{0:T(512)(128)(4,1)} %bitcast.5, pred[1]{0:T(512)(128)(4,1)} %bitcast.4, pred[1]{0:T(512)(128)(4,1)} %bitcast.2, pred[1]{0:T(512)(128)(4,1)} %bitcast.1), kind=kLoop, calls=%fused_computation | loop fusion | flops 16 | bytes 20 | tf_op jit(solution)/shard_map/convert_element_type | solution.py:441
  4.6 0.0 copy-start
  4.6 1.1 %copy-done = bf16[1,1,128,3072]{3,2,1,0:T(8,128)(2,1)S(1)} copy-done((bf16[1,1,128,3072]{3,2,1,0:T(8,128)(2,1)S(1)}, bf16[1,1,128,3072]{3,2,1,0:T(8,128)(2,1)}, u32[]{:S(2)}) %copy-start) | copy-done | bytes 786456
  5.8 0.0 copy-start.1
  5.8 1.0 copy-done.1
  6.8 0.0 copy-start.2
  6.8 1.0 copy-done.2
  7.9 0.0 copy-start.3
  7.9 1.0 copy-done.3
  8.9 0.0 copy-start.4
  8.9 1.0 copy-done.4
  9.9 98.4 %shard_map.93 = (bf16[128,2048]{1,0:T(8,128)(2,1)S(1)}, bf16[128,2048]{1,0:T(8,128)(2,1)S(1)}, bf16[128,2048]{1,0:T(8,128)(2,1)S(1)}, f32[256,96]{1,0:T(8,128)S(1)}) custom-call(f32[4]{0:T(128)S(1)} %add_convert_fusion.flags, bf16[128,2048]{1,0:T(8,128)(2,1)S(1)} %bitcast.27, bf16[128,2048]{1,0:T(8,128)(2,1)S(1)} %bitcast.28, ...), custom_call_target="tpu_custom_call" | custom-call | tf_op jit(solution)/shard_map/pallas_call | solution.py:446
  108.3 0.7 copy.10
  109.0 0.8 copy.14
  109.8 0.8 copy.15
  110.6 0.8 copy.16
Async XLA Ops:
  0.6 0.7 copy-start.5
  4.6 1.1 %copy-start = (bf16[1,1,128,3072]{3,2,1,0:T(8,128)(2,1)S(1)}, bf16[1,1,128,3072]{3,2,1,0:T(8,128)(2,1)}, u32[]{:S(2)}) copy-start(bf16[1,1,128,3072]{3,2,1,0:T(8,128)(2,1)} %param.10) | copy-start | bytes 2359300
  5.8 1.0 copy-start.1
  6.8 1.0 copy-start.2
  7.9 1.0 copy-start.3
  8.9 1.0 copy-start.4

commit v2 on v1

v2 whole, which is shorter than its diff:
```python
import functools

import jax
import jax.numpy as jnp
from jax import lax
from jax.experimental import pallas as pl
from jax.experimental.pallas import tpu as pltpu
from jax.sharding import PartitionSpec as P

D = 3072
HEAD_DIM = 128
NS_STEPS = 5
MESH = pl.DeviceIdType.MESH
F32 = jnp.float32
BF16 = jnp.bfloat16
BEST = lax.Precision.HIGHEST

coeff_a = 3.4445
coeff_b = -4.775
coeff_c = 2.0315

NT = (((1,), (1,)), ((), ()))
NN = (((1,), (0,)), ((), ()))
TN = (((0,), (0,)), ((), ()))


def mm(a, b, dims):
    return lax.dot_general(a, b, dims, preferred_element_type=F32)


def mmh(a, b, dims=NN):
    return lax.dot_general(a, b, dims, precision=BEST, preferred_element_type=F32)


def head_grads(q, kk, vv, do):
    score_scale = HEAD_DIM ** (-0.5)
    scores = mm(q, kk, NT) * score_scale
    row_max = jnp.max(scores, axis=1, keepdims=True)
    exp_scores = jnp.exp(scores - row_max)
    weights = exp_scores / jnp.sum(exp_scores, axis=1, keepdims=True)
    weights_b = weights.astype(BF16)
    attended = mm(weights_b, vv, NN).astype(BF16)
    delta = jnp.sum(do.astype(F32) * attended.astype(F32), axis=1, keepdims=True)
    dweights = mm(do, vv, NT)
    dscore_b = (weights * (dweights - delta)).astype(BF16)
    dq = (mm(dscore_b, kk, NN) * score_scale).astype(BF16)
    dk = mm(dscore_b, q, TN) * score_scale
    dv = mm(weights_b, do, TN)
    return dq, dk, dv, attended


def kernel(
    geo,
    nb,
    q_hbm, k_hbm, v_hbm, do_hbm, proj_hbm,
    dq_hbm, dk_hbm, dv_hbm, upd_hbm,
    q_v, k_v, v_v, do_v,
    dq_v, dk_v, dv_v, upd_v,
    halo, far_out, far_in, own_k, own_v,
    proj_all, proj_t, att, part, rx, xsum, rz,
    g_part, g_pair, g_mine, g_in, g_full, poly_all,
    in_sem, out_sem,
    halo_s, halo_r, far_s, far_r,
    proj_s, proj_r,
    att_s, att_r, fwd_s, fwd_r, x_s, x_r, z_s, z_r,
    pair_s, pair_r, g1_s, g1_r, g2_s, g2_r,
):
    nz, ny, nx = geo
    seq = ny * nx * 2
    chips = ny * nx
    hc = nz // 2
    tile = q_v.shape[0]
    cb = 2 * HEAD_DIM
    qcols = proj_all.shape[2]
    xcols = qcols // nx
    ccols = xcols // 2
    z = lax.axis_index("dp")
    s = lax.axis_index("seq")
    c = lax.rem(s, 2)
    chip = s // 2
    x = lax.rem(chip, nx)
    y = chip // nx
    a = lax.rem(y, 2)
    b = y // 2
    zrow = z // 2
    zhalf = lax.rem(z, 2)
    right = (z, lax.rem(s + 1, seq))
    left = (z, lax.rem(s + seq - 1, seq))
    other_core = (z, chip * 2 + 1 - c)

    def at(yy, xx, cc):
        return (z, (yy * nx + xx) * 2 + cc)

    def y_off(d):
        return lax.rem(y + d, ny)

    def core_off(e):
        return 1 - c if e else c

    def block_of(i, half):
        return 2 * lax.rem(zrow + i, hc) + half

    def lanes(block):
        return pl.ds(pl.multiple_of(block * cb, cb), cb)

    def remote(src, dst, ss, rs, dev):
        return pltpu.make_async_remote_copy(
            src_ref=src, dst_ref=dst, send_sem=ss, recv_sem=rs,
            device_id=dev, device_id_type=MESH,
        )

    def quarter_cols(quarter):
        return pl.ds(pl.multiple_of(quarter * qcols, qcols), qcols)

    loads = [
        pltpu.make_async_copy(k_hbm, k_v, in_sem.at[1]),
        pltpu.make_async_copy(v_hbm, v_v, in_sem.at[2]),
        pltpu.make_async_copy(q_hbm, q_v, in_sem.at[0]),
        pltpu.make_async_copy(do_hbm, do_v, in_sem.at[3]),
        pltpu.make_async_copy(
            proj_hbm.at[:, quarter_cols(2 * b + c)], proj_all.at[0], in_sem.at[4]
        ),
    ]
    for load in loads:
        load.start()

    barrier = pltpu.get_barrier_semaphore()

    def greet(dev):
        pl.semaphore_signal(barrier, inc=1, device_id=dev, device_id_type=MESH)

    def chip_off(r):
        return lax.rem(chip + r, chips)

    for r in range(1, chips):
        greet((z, chip_off(r) * 2 + c))
    for d in range(ny):
        greet(at(y_off(d), x, 1 - c))
    greet(right)
    greet(left)
    for r in range(1, nz):
        zz = lax.rem(z + r, nz)
        greet((zz, ((2 * b + zhalf) * nx + x) * 2 + a))

    def greet_targets(step, carry):
        zz = block_of(step, a)
        for cc in range(2):
            greet((zz, ((2 * b + c) * nx + x) * 2 + cc))
        return carry

    skip = jnp.where(a == zhalf, 1, 0)
    lax.fori_loop(skip, hc, greet_targets, 0)
    pl.semaphore_wait(barrier, chips - 1 + ny + 2 + nz - 1 + 2 * (hc - skip))

    def halo_copy(i, half, kv, way):
        t = 2 * i + half
        src = (k_hbm, v_hbm)[kv].at[:, lanes(block_of(i, half))]
        return remote(
            src, halo.at[way, kv, t], halo_s.at[way, kv, t], halo_r.at[way, kv, t],
            (right, left)[way],
        )

    def start_halo(i, carry):
        for half in range(2):
            for kv in range(2):
                for way in range(2):
                    halo_copy(i, half, kv, way).start()
        return carry

    lax.fori_loop(0, hc, start_halo, 0)

    others = [(d, e) for d in range(ny) for e in range(2) if d + e > 0]

    def proj_copy(d, e):
        yy, cc = y_off(d), core_off(e)
        slot = 2 * d + e
        return remote(
            proj_hbm.at[:, quarter_cols(2 * (yy // 2) + cc)], proj_all.at[slot],
            proj_s.at[slot], proj_r.at[slot], at(yy, x, cc),
        )

    for d, e in others:
        proj_copy(d, e).start()
    for load in loads:
        load.wait()

    def mask(condition):
        return jnp.where(condition, jnp.float32(1.0), jnp.float32(0.0))

    go_left = mask(nb[0, s] < s)
    go_right = 1.0 - go_left
    left_sends = mask(nb[0, jnp.maximum(s - 1, 0)] == s)
    right_sends = mask(nb[0, jnp.minimum(s + 1, seq - 1)] == s)

    def att_copy(i, d):
        half = a if d % 2 == 0 else 1 - a
        return remote(
            far_out.at[2, 2 * i + half], att.at[i, pl.ds(2 * d * tile, tile)],
            att_s.at[i, d], att_r.at[i, d], at(y_off(d), x, c),
        )

    def fwd_copy(i, d):
        src = far_out.at[2, 2 * i + a] if d == 0 else att.at[i, pl.ds(2 * d * tile, tile)]
        return remote(
            src, att.at[i, pl.ds((2 * d + 1) * tile, tile)],
            fwd_s.at[i, d], fwd_r.at[i, d], other_core,
        )

    def far_copy(i, half, kv, way):
        t = 2 * i + half
        return remote(
            far_out.at[kv, t], far_in.at[way, kv, t], far_s.at[way, kv, t],
            far_r.at[way, kv, t], (right, left)[way],
        )

    turns_right = (x == nx - 1) & (c == 1)
    turns_left = (x == 0) & (c == 0)

    def start_far(i, half, late):
        for way in range(2):
            turns = (turns_right, turns_left)[way]

            @pl.when(turns if late else ~turns)
            def _():
                for kv in range(2):
                    far_copy(i, half, kv, way).start()

    def attend(i, carry):
        for half in range(2):
            t = 2 * i + half
            block = block_of(i, half)
            for kv in range(2):
                for way in range(2):
                    halo_copy(i, half, kv, way).wait_recv()
            for h in range(2):
                inside = pl.ds(h * HEAD_DIM, HEAD_DIM)
                cols = pl.ds(
                    pl.multiple_of(block * cb + h * HEAD_DIM, HEAD_DIM), HEAD_DIM
                )

                def beside(kv):
                    from_left = halo[0, kv, t, :, inside].astype(F32) * go_left
                    from_right = halo[1, kv, t, :, inside].astype(F32) * go_right
                    return (from_left + from_right).astype(BF16)

                q = q_v[:, cols]
                do = do_v[:, cols]
                kk = jnp.concatenate([k_v[:, cols], beside(0)], 0)
                vv = jnp.concatenate([v_v[:, cols], beside(1)], 0)
                dq, dk, dv, attended = head_grads(q, kk, vv, do)
                dq_v[:, cols] = dq
                own_k[:, cols] = dk[:tile]
                own_v[:, cols] = dv[:tile]
                far_out[0, t, :, inside] = dk[tile:].astype(BF16)
                far_out[1, t, :, inside] = dv[tile:].astype(BF16)
                far_out[2, t, :, inside] = attended

            @pl.when(a == half)
            def _():
                att[i, pl.ds(0, tile)] = far_out[2, t]
                fwd_copy(i, 0).start()

            start_far(i, half, False)
        return carry

    lax.fori_loop(0, hc, attend, 0)
    dq_out = pltpu.make_async_copy(dq_v, dq_hbm, out_sem.at[0])
    dq_out.start()

    def send_att(i):
        for d in range(1, ny):
            att_copy(i, d).start()

    ahead = 2
    for i in range(min(ahead, hc)):
        send_att(i)

    def turn(slot):
        proj_t[:, slot * tile : (slot + 1) * tile] = proj_all[slot].T

    turn(0)
    for d, e in others:
        proj_copy(d, e).wait_recv()
        turn(2 * d + e)

    def x_copy(i, d):
        xx = lax.rem(x + d, nx)
        rows = pl.ds(pl.multiple_of(xx * xcols, xcols), xcols)
        return remote(
            part.at[i, rows], rx.at[i, d], x_s.at[i, d], x_r.at[i, d], at(y, xx, c)
        )

    def z_copy(i, e):
        zz = block_of(i, a)
        cc = core_off(e)
        rows = pl.ds(pl.multiple_of(cc * ccols, ccols), ccols)
        slot = lax.rem(zz - z + nz, nz)
        return remote(
            xsum.at[i, rows], rz.at[slot], z_s.at[i, e], z_r.at[slot],
            (zz, ((2 * b + c) * nx + x) * 2 + cc),
        )

    def stays(i):
        return (block_of(i, a) == z) & (c == a)

    def forward(i):
        for d in range(1, ny):
            att_copy(i, d).wait_recv()
            fwd_copy(i, d).start()

        @pl.when(i + ahead < hc)
        def _():
            send_att(i + ahead)

    def product(i):
        for d in range(ny):
            fwd_copy(i, d).wait_recv()
        part[i] = mm(proj_t[...], att[i], NN).astype(BF16)
        for d in range(1, nx):
            x_copy(i, d).start()

    def add_x(i):
        mine = pl.ds(pl.multiple_of(x * xcols, xcols), xcols)
        total = part[i, mine].astype(F32)
        for d in range(1, nx):
            x_copy(i, d).wait_recv()
            total = total + rx[i, d].astype(F32)
        xsum[i] = total.astype(BF16)
        here = stays(i)

        @pl.when(here)
        def _():
            rz[0] = xsum[i, pl.ds(pl.multiple_of(c * ccols, ccols), ccols)]

        @pl.when(~here)
        def _():
            z_copy(i, 0).start()

        z_copy(i, 1).start()

    def step(i, carry):
        @pl.when(i < hc)
        def _():
            forward(i)

        @pl.when(i > 0)
        def _():
            product(i - 1)

        return carry

    lax.fori_loop(0, hc + 1, step, 0)

    def sums(i, carry):
        add_x(i)
        return carry

    lax.fori_loop(0, hc, sums, 0)

    def late_far(i, carry):
        for half in range(2):
            start_far(i, half, True)
        return carry

    lax.fori_loop(0, hc, late_far, 0)

    def rz_copy(slot):
        return remote(rz.at[slot], rz.at[slot], z_s.at[0, 1], z_r.at[slot], right)

    @pl.when(~((zhalf == a) & (c == a)))
    def _():
        rz_copy(0).wait_recv()

    grad = rz[0].astype(F32)
    for slot in range(1, nz):
        rz_copy(slot).wait_recv()
        grad = grad + rz[slot].astype(F32)

    piece = HEAD_DIM // chips
    for h in range(2):
        part_h = grad[:, h * HEAD_DIM : (h + 1) * HEAD_DIM]
        g_part[h] = mmh(part_h, part_h, TN)
    pair = remote(
        g_part.at[1 - c], g_pair, pair_s.at[0], pair_r.at[0], other_core
    )
    pair.start()
    pair.wait_recv()
    g_mine[...] = g_part[c] + g_pair[...]

    def rows_of(index):
        return pl.ds(pl.multiple_of(index * piece, piece), piece)

    def g1_copy(r):
        there = chip_off(r)
        return remote(
            g_mine.at[rows_of(there)], g_in.at[r], g1_s.at[r], g1_r.at[r],
            (z, there * 2 + c),
        )

    def g2_copy(r):
        return remote(
            g_full.at[rows_of(chip)], g_full.at[rows_of(chip)], g2_s.at[r],
            g2_r.at[r], (z, chip_off(r) * 2 + c),
        )

    def g2_from(r):
        source = rows_of(lax.rem(chip + chips - r, chips))
        return remote(
            g_full.at[source], g_full.at[source], g2_s.at[r], g2_r.at[r], right
        )

    for r in range(1, chips):
        g1_copy(r).start()
    total = g_mine[rows_of(chip)]
    for r in range(1, chips):
        g1_copy(r).wait_recv()
        total = total + g_in[r]
    g_full[rows_of(chip)] = total
    for r in range(1, chips):
        g2_copy(r).start()

    def gather_far(i, carry):
        for half in range(2):
            t = 2 * i + half
            cols = lanes(block_of(i, half))
            for kv in range(2):
                for way in range(2):
                    far_copy(i, half, kv, way).wait_recv()
                out = (dk_v, dv_v)[kv]
                out[:, cols] = (
                    (own_k, own_v)[kv][:, cols]
                    + far_in[0, kv, t].astype(F32) * left_sends
                    + far_in[1, kv, t].astype(F32) * right_sends
                ).astype(BF16)
        return carry

    lax.fori_loop(0, hc, gather_far, 0)
    dk_out = pltpu.make_async_copy(dk_v, dk_hbm, out_sem.at[1])
    dv_out = pltpu.make_async_copy(dv_v, dv_hbm, out_sem.at[2])
    dk_out.start()
    dv_out.start()

    for r in range(1, chips):
        g2_from(r).wait_recv()

    row_id = lax.broadcasted_iota(jnp.int32, (HEAD_DIM, HEAD_DIM), 0)
    col_id = lax.broadcasted_iota(jnp.int32, (HEAD_DIM, HEAD_DIM), 1)
    eye = jnp.where(row_id == col_id, 1.0, 0.0).astype(F32)
    gram = g_full[...]
    trace = jnp.sum(jnp.sum(gram * eye, axis=1, keepdims=True), axis=0, keepdims=True)
    norm = jnp.sqrt(trace) + 1e-07
    gram = gram / norm / norm
    whole = None
    for turn_id in range(NS_STEPS):
        poly = coeff_a * eye + coeff_b * gram + coeff_c * mmh(gram, gram)
        if turn_id < NS_STEPS - 1:
            gram = mmh(mmh(poly, gram), poly)
        whole = poly if whole is None else mmh(poly, whole)
    poly_all[c] = whole / norm
    swap = remote(
        poly_all.at[c], poly_all.at[c], pair_s.at[1], pair_r.at[1], other_core
    )
    swap.start()
    remote(
        poly_all.at[1 - c], poly_all.at[1 - c], pair_s.at[1], pair_r.at[1], other_core
    ).wait_recv()
    for h in range(2):
        part_h = grad[:, h * HEAD_DIM : (h + 1) * HEAD_DIM]
        result = mmh(part_h, poly_all[h], NT)
        upd_v[:, h * HEAD_DIM : (h + 1) * HEAD_DIM] = result * (0.2 * D**0.5)
    upd_out = pltpu.make_async_copy(upd_v, upd_hbm, out_sem.at[3])
    upd_out.start()

    def drain(i, carry):
        for half in range(2):
            for kv in range(2):
                for way in range(2):
                    halo_copy(i, half, kv, way).wait_send()
                    far_copy(i, half, kv, way).wait_send()
        for d in range(ny):
            if d > 0:
                att_copy(i, d).wait_send()
            fwd_copy(i, d).wait_send()
        for d in range(1, nx):
            x_copy(i, d).wait_send()

        @pl.when(~stays(i))
        def _():
            z_copy(i, 0).wait_send()

        z_copy(i, 1).wait_send()
        return carry

    lax.fori_loop(0, hc, drain, 0)
    for d, e in others:
        proj_copy(d, e).wait_send()
    pair.wait_send()
    swap.wait_send()
    for r in range(1, chips):
        g1_copy(r).wait_send()
        g2_copy(r).wait_send()
    for out in (dq_out, dk_out, dv_out, upd_out):
        out.wait()


def settle_kernel(*refs):
    count = (len(refs) - 2) // 3
    ins, outs, kept = refs[:count], refs[count : 2 * count], refs[2 * count : 3 * count]
    in_sem, out_sem = refs[-2:]
    loads = [
        pltpu.make_async_copy(ins[n], kept[n], in_sem.at[n]) for n in range(count)
    ]
    stores = [
        pltpu.make_async_copy(kept[n], outs[n], out_sem.at[n]) for n in range(count)
    ]
    for load in loads:
        load.start()
    for load, store in zip(loads, stores):
        load.wait()
        store.start()
    for store in stores:
        store.wait()


def settle(*arrays):
    anyspec = pl.BlockSpec(memory_space=pl.ANY)
    sems = pltpu.SemaphoreType.DMA((len(arrays),))
    return pl.pallas_call(
        settle_kernel,
        out_shape=tuple(jax.ShapeDtypeStruct(a.shape, a.dtype) for a in arrays),
        in_specs=[anyspec] * len(arrays),
        out_specs=(anyspec,) * len(arrays),
        scratch_shapes=[pltpu.VMEM(a.shape, a.dtype) for a in arrays] + [sems, sems],
        compiler_params=pltpu.CompilerParams(vmem_limit_bytes=60 * 2**20),
    )(*arrays)


def local(geo, query_tiles, key_tiles, value_tiles, attn_grad, proj_grad, neighbour):
    nz, ny, nx = geo
    seq = ny * nx * 2
    hc = nz // 2
    tile, width = query_tiles.shape[2:]
    depth = proj_grad.shape[3]
    qcols = depth // ny
    xcols = qcols // nx
    cb = 2 * HEAD_DIM
    group = ny * 2
    anyspec = pl.BlockSpec(memory_space=pl.ANY)
    chips = seq // 2
    rows = jax.ShapeDtypeStruct((tile, width), BF16)
    dma = pltpu.SemaphoreType.DMA
    halves = (2, 2, 2 * hc)
    square = (HEAD_DIM, HEAD_DIM)
    out = pl.pallas_call(
        functools.partial(kernel, geo),
        out_shape=(rows, rows, rows, jax.ShapeDtypeStruct((depth // seq, cb), F32)),
        in_specs=[pl.BlockSpec(memory_space=pltpu.SMEM)] + [anyspec] * 5,
        out_specs=(anyspec,) * 4,
        scratch_shapes=[pltpu.VMEM((tile, width), BF16)] * 7
        + [
            pltpu.VMEM((depth // seq, cb), F32),
            pltpu.VMEM(halves + (tile, cb), BF16),
            pltpu.VMEM((3, 2 * hc, tile, cb), BF16),
            pltpu.VMEM(halves + (tile, cb), BF16),
            pltpu.VMEM((tile, width), F32),
            pltpu.VMEM((tile, width), F32),
            pltpu.VMEM((group, tile, qcols), BF16),
            pltpu.VMEM((qcols, group * tile), BF16),
            pltpu.VMEM((hc, group * tile, cb), BF16),
            pltpu.VMEM((hc, qcols, cb), BF16),
            pltpu.VMEM((hc, nx, xcols, cb), BF16),
            pltpu.VMEM((hc, xcols, cb), BF16),
            pltpu.VMEM((nz, xcols // 2, cb), BF16),
            pltpu.VMEM((2,) + square, F32),
            pltpu.VMEM(square, F32),
            pltpu.VMEM(square, F32),
            pltpu.VMEM((chips, HEAD_DIM // chips, HEAD_DIM), F32),
            pltpu.VMEM(square, F32),
            pltpu.VMEM((2,) + square, F32),
            dma((5,)), dma((4,)),
            dma(halves), dma(halves), dma(halves), dma(halves),
            dma((group,)), dma((group,)),
            dma((hc, ny)), dma((hc, ny)), dma((hc, ny)), dma((hc, ny)),
            dma((hc, nx)), dma((hc, nx)), dma((hc, 2)), dma((nz,)),
            dma((2,)), dma((2,)),
            dma((chips,)), dma((chips,)), dma((chips,)), dma((chips,)),
        ],
        compiler_params=pltpu.CompilerParams(
            collective_id=0, has_side_effects=True, vmem_limit_bytes=60 * 2**20
        ),
    )(
        neighbour, query_tiles[0, 0], key_tiles[0, 0], value_tiles[0, 0],
        attn_grad[0, 0], proj_grad[0, 0],
    )
    dq, dk, dv, upd = settle(*out)
    return dq[None, None], dk[None, None], dv[None, None], upd.T


def solution(mesh):
    nz, seq = mesh.shape["dp"], mesh.shape["seq"]
    nx = 4 if seq == 32 else 2
    geo = (nz, seq // (2 * nx), nx)
    tiled = P("dp", "seq", None, None)
    return jax.shard_map(
        functools.partial(local, geo),
        mesh=mesh,
        in_specs=(tiled, tiled, tiled, tiled, tiled, P("dp", None)),
        out_specs=(tiled, tiled, tiled, P("dp", "seq")),
        check_vma=False,
    )
```

time: 112 us -> 96.9 us (0.87)
  local copies, waits for them, and re-layouts: 9.06 us -> 0 us
  Pallas kernels: 98.4 us -> 95.7 us
  other arithmetic: 2.69 us -> 0 us
    unnamed x16 -> x0, local copies, waits for them, and re-layouts: 9.06 us -> none
    pallas_call x1, Pallas kernels: 98.4 us -> 93.5 us  [local(): pl.pallas_call(functools.partial(kernel, geo), out_shape=(rows, rows, row...]
    pallas_call x0 -> x1, Pallas kernels: none -> 2.27 us  [settle(): pl.pallas_call(settle_kernel, out_shape=tuple((jax.ShapeDtypeStruct(a.sha...]
    convert_element_type x1 -> x0, other arithmetic: 2.02 us -> none  [local(): flags = jnp.stack([go_left, ~go_left, left_sends, right_sends]).astype(F32)]
where the time goes in v2:
time: 96.9 us; the launch traced here: 96.4 us
  Pallas kernels  95.7 us (99%)
    pallas_call x1, Pallas kernels, local(): pl.pallas_call(functools.partial(kernel, geo), out_shape=(rows, rows, row...  93.5 us
    pallas_call x1, Pallas kernels, settle(): pl.pallas_call(settle_kernel, out_shape=tuple((jax.ShapeDtypeStruct(a.sha...  2.27 us

profile of v2, /device:TPU:1, one launch (start us, length us, event | category | flops | bytes accessed | tf_op | source)
XLA Modules:
  0.0 96.4 jit_solution(879885321188169067)
XLA Ops:
  0.6 93.5 %shard_map.93 = (bf16[128,2048]{1,0:T(8,128)(2,1)}, bf16[128,2048]{1,0:T(8,128)(2,1)}, bf16[128,2048]{1,0:T(8,128)(2,1)}, f32[96,256]{1,0:T(8,128)}) custom-call(s32[1,32]{1,0:T(1,128)} %nb.1, bf16[128,2048]{1,0:T(8,128)(2,1)} %bitcast.10, bf16[128,2048]{1,0:T(8,128)(2,1)} %bitcast.11, bf16[128,2048]{1,0:T(8,128)(2,1)} %bitcast.12, ...), custom_call_target="tpu_custom_call" | custom-call | tf_op jit(solution)/shard_map/pallas_call | solution.py:554
  94.1 2.3 %shard_map.94 = (bf16[128,2048]{1,0:T(8,128)(2,1)}, bf16[128,2048]{1,0:T(8,128)(2,1)}, bf16[128,2048]{1,0:T(8,128)(2,1)}, f32[96,256]{1,0:T(8,128)}) custom-call(bf16[128,2048]{1,0:T(8,128)(2,1)} %get-tuple-element.12.refs_0_, bf16[128,2048]{1,0:T(8,128)(2,1)} %get-tuple-element.13.refs_1_, bf16[128,2048]{1,0:T(8,128)(2,1)} %get-tuple-element.14.refs_2_, ...), custom_call_target="tpu_custom_call" | custom-call | tf_op jit(solution)/shard_map/pallas_call | solution.py:528

commit v3 on v2

--- a/solution.py
+++ b/solution.py
@@ -57,12 +57,12 @@
     q_v, k_v, v_v, do_v,
     dq_v, dk_v, dv_v, upd_v,
     halo, far_out, far_in, own_k, own_v,
-    proj_all, proj_t, att, part, rx, xsum, rz,
+    proj_all, proj_t, att, part, rx1, sum1, rx2, sum2, rz,
     g_part, g_pair, g_mine, g_in, g_full, poly_all,
     in_sem, out_sem,
     halo_s, halo_r, far_s, far_r,
     proj_s, proj_r,
-    att_s, att_r, fwd_s, fwd_r, x_s, x_r, z_s, z_r,
+    att_s, att_r, s1_s, s1_r, s2_s, s2_r, z_s, z_r,
     pair_s, pair_r, g1_s, g1_r, g2_s, g2_r,
 ):
     nz, ny, nx = geo
@@ -71,19 +71,17 @@
     hc = nz // 2
     tile = q_v.shape[0]
     cb = 2 * HEAD_DIM
-    qcols = proj_all.shape[2]
-    xcols = qcols // nx
-    ccols = xcols // 2
+    hcols = proj_all.shape[2]
+    ys = ny // 2
+    ccols = hcols // chips
     z = lax.axis_index("dp")
     s = lax.axis_index("seq")
     c = lax.rem(s, 2)
     chip = s // 2
     x = lax.rem(chip, nx)
     y = chip // nx
-    a = lax.rem(y, 2)
-    b = y // 2
-    zrow = z // 2
-    zhalf = lax.rem(z, 2)
+    p = lax.rem(z, 2)
+    zp = z // 2
     right = (z, lax.rem(s + 1, seq))
     left = (z, lax.rem(s + seq - 1, seq))
     other_core = (z, chip * 2 + 1 - c)
@@ -91,14 +89,14 @@
     def at(yy, xx, cc):
         return (z, (yy * nx + xx) * 2 + cc)
 
+    def mate(cc):
+        return (z + 1 - 2 * p, chip * 2 + cc)
+
     def y_off(d):
         return lax.rem(y + d, ny)
 
-    def core_off(e):
-        return 1 - c if e else c
-
     def block_of(i, half):
-        return 2 * lax.rem(zrow + i, hc) + half
+        return 2 * lax.rem(zp + i, hc) + half
 
     def lanes(block):
         return pl.ds(pl.multiple_of(block * cb, cb), cb)
@@ -109,8 +107,8 @@
             device_id=dev, device_id_type=MESH,
         )
 
-    def quarter_cols(quarter):
-        return pl.ds(pl.multiple_of(quarter * qcols, qcols), qcols)
+    def half_cols(half):
+        return pl.ds(pl.multiple_of(half * hcols, hcols), hcols)
 
     loads = [
         pltpu.make_async_copy(k_hbm, k_v, in_sem.at[1]),
@@ -118,7 +116,7 @@
         pltpu.make_async_copy(q_hbm, q_v, in_sem.at[0]),
         pltpu.make_async_copy(do_hbm, do_v, in_sem.at[3]),
         pltpu.make_async_copy(
-            proj_hbm.at[:, quarter_cols(2 * b + c)], proj_all.at[0], in_sem.at[4]
+            proj_hbm.at[:, half_cols(p)], proj_all.at[0], in_sem.at[4]
         ),
     ]
     for load in loads:
@@ -132,25 +130,31 @@
     def chip_off(r):
         return lax.rem(chip + r, chips)
 
+    def owner(i):
+        return (block_of(i, c), (((p * ys + y // 2) * nx) + x) * 2 + lax.rem(y, 2))
+
+    stays = (c == p) & (p * ys + y // 2 == y) & (lax.rem(y, 2) == c)
+
     for r in range(1, chips):
         greet((z, chip_off(r) * 2 + c))
-    for d in range(ny):
-        greet(at(y_off(d), x, 1 - c))
+    greet(other_core)
+    greet(mate(c))
+    greet(mate(1 - c))
     greet(right)
     greet(left)
-    for r in range(1, nz):
-        zz = lax.rem(z + r, nz)
-        greet((zz, ((2 * b + zhalf) * nx + x) * 2 + a))
-
-    def greet_targets(step, carry):
-        zz = block_of(step, a)
-        for cc in range(2):
-            greet((zz, ((2 * b + c) * nx + x) * 2 + cc))
-        return carry
-
-    skip = jnp.where(a == zhalf, 1, 0)
-    lax.fori_loop(skip, hc, greet_targets, 0)
-    pl.semaphore_wait(barrier, chips - 1 + ny + 2 + nz - 1 + 2 * (hc - skip))
+    source_chip = (2 * lax.rem(y, ys) + c) * nx + x
+    for m in range(1, hc):
+        greet(owner(m))
+        greet((2 * lax.rem(zp + m, hc) + y // ys, source_chip * 2 + p))
+
+    @pl.when(~stays)
+    def _():
+        greet(owner(0))
+        greet((2 * zp + y // ys, source_chip * 2 + p))
+
+    pl.semaphore_wait(
+        barrier, chips - 1 + 5 + 2 * (hc - 1) + jnp.where(stays, 0, 2)
+    )
 
     def halo_copy(i, half, kv, way):
         t = 2 * i + half
@@ -169,18 +173,18 @@
 
     lax.fori_loop(0, hc, start_halo, 0)
 
-    others = [(d, e) for d in range(ny) for e in range(2) if d + e > 0]
-
-    def proj_copy(d, e):
-        yy, cc = y_off(d), core_off(e)
-        slot = 2 * d + e
+    def proj_copy(slot):
+        if slot == 3:
+            src = proj_all.at[2]
+        else:
+            src = proj_hbm.at[:, half_cols(p if slot == 1 else 1 - p)]
         return remote(
-            proj_hbm.at[:, quarter_cols(2 * (yy // 2) + cc)], proj_all.at[slot],
-            proj_s.at[slot], proj_r.at[slot], at(yy, x, cc),
-        )
-
-    for d, e in others:
-        proj_copy(d, e).start()
+            src, proj_all.at[slot], proj_s.at[slot], proj_r.at[slot],
+            mate(c) if slot == 2 else other_core,
+        )
+
+    proj_copy(2).start()
+    proj_copy(1).start()
     for load in loads:
         load.wait()
 
@@ -192,18 +196,12 @@
     left_sends = mask(nb[0, jnp.maximum(s - 1, 0)] == s)
     right_sends = mask(nb[0, jnp.minimum(s + 1, seq - 1)] == s)
 
-    def att_copy(i, d):
-        half = a if d % 2 == 0 else 1 - a
+    def att_copy(i, slot):
+        half = c if slot == 2 else 1 - c
         return remote(
-            far_out.at[2, 2 * i + half], att.at[i, pl.ds(2 * d * tile, tile)],
-            att_s.at[i, d], att_r.at[i, d], at(y_off(d), x, c),
-        )
-
-    def fwd_copy(i, d):
-        src = far_out.at[2, 2 * i + a] if d == 0 else att.at[i, pl.ds(2 * d * tile, tile)]
-        return remote(
-            src, att.at[i, pl.ds((2 * d + 1) * tile, tile)],
-            fwd_s.at[i, d], fwd_r.at[i, d], other_core,
+            far_out.at[2, 2 * i + half], att.at[i, pl.ds(slot * tile, tile)],
+            att_s.at[i, slot], att_r.at[i, slot],
+            (None, other_core, mate(c), mate(1 - c))[slot],
         )
 
     def far_copy(i, half, kv, way):
@@ -213,19 +211,65 @@
             far_r.at[way, kv, t], (right, left)[way],
         )
 
-    turns_right = (x == nx - 1) & (c == 1)
-    turns_left = (x == 0) & (c == 0)
-
-    def start_far(i, half, late):
+    def start_far(i, half):
         for way in range(2):
-            turns = (turns_right, turns_left)[way]
-
-            @pl.when(turns if late else ~turns)
+            for kv in range(2):
+                far_copy(i, half, kv, way).start()
+
+    def turn(slot):
+        turned = proj_all[slot].T
+        for yy in range(ny):
+            for xx in range(nx):
+                start = (((yy // 2) * nx + xx) * 2 + yy % 2) * ccols
+                place = (yy * nx + xx) * ccols
+                proj_t[place : place + ccols, slot * tile : (slot + 1) * tile] = turned[
+                    start : start + ccols
+                ]
+
+    def turn_all():
+        turn(0)
+        turn(2)
+        for slot in (1, 3):
+            proj_copy(slot).wait_recv()
+            turn(slot)
+
+    def first_copy(i, d):
+        if i % 2 == 0:
+            xx = lax.rem(x + d, nx)
+            src, dev = part.at[i, :, xx], at(y, xx, c)
+        else:
+            src, dev = part.at[i, y_off(d)], at(y_off(d), x, c)
+        return remote(src, rx1.at[i, d], s1_s.at[i, d], s1_r.at[i, d], dev)
+
+    def second_copy(i, d):
+        if i % 2 == 0:
+            src, dev = sum1.at[i, y_off(d)], at(y_off(d), x, c)
+        else:
+            xx = lax.rem(x + d, nx)
+            src, dev = sum1.at[i, xx], at(y, xx, c)
+        return remote(src, rx2.at[i, d], s2_s.at[i, d], s2_r.at[i, d], dev)
+
+    def z_copy(i):
+        return remote(sum2.at[i], rz.at[i], z_s.at[i], z_r.at[i], owner(i))
+
+    def product(i):
+        for slot in range(1, 4):
+            att_copy(i, slot).wait_recv()
+        part[i] = mm(proj_t[...], att[i], NN).astype(BF16).reshape(part.shape[1:])
+        for d in range(1, nx if i % 2 == 0 else ny):
+            first_copy(i, d).start()
+
+    early = min(2, hc - 1)
+
+    def attend(i, carry):
+        if early:
+
+            @pl.when(i == hc - 1)
             def _():
-                for kv in range(2):
-                    far_copy(i, half, kv, way).start()
-
-    def attend(i, carry):
+                turn_all()
+                for k in range(early):
+                    product(k)
+
         for half in range(2):
             t = 2 * i + half
             block = block_of(i, half)
@@ -255,126 +299,73 @@
                 far_out[1, t, :, inside] = dv[tile:].astype(BF16)
                 far_out[2, t, :, inside] = attended
 
-            @pl.when(a == half)
+            @pl.when(c == half)
             def _():
+                att_copy(i, 2).start()
                 att[i, pl.ds(0, tile)] = far_out[2, t]
-                fwd_copy(i, 0).start()
-
-            start_far(i, half, False)
+
+            @pl.when(c != half)
+            def _():
+                att_copy(i, 3).start()
+                att_copy(i, 1).start()
+
+        @pl.when(i == max(hc - 2, 0))
+        def _():
+            proj_copy(2).wait_recv()
+            proj_copy(3).start()
+
         return carry
 
     lax.fori_loop(0, hc, attend, 0)
     dq_out = pltpu.make_async_copy(dq_v, dq_hbm, out_sem.at[0])
     dq_out.start()
 
-    def send_att(i):
-        for d in range(1, ny):
-            att_copy(i, d).start()
-
-    ahead = 2
-    for i in range(min(ahead, hc)):
-        send_att(i)
-
-    def turn(slot):
-        proj_t[:, slot * tile : (slot + 1) * tile] = proj_all[slot].T
-
-    turn(0)
-    for d, e in others:
-        proj_copy(d, e).wait_recv()
-        turn(2 * d + e)
-
-    def x_copy(i, d):
-        xx = lax.rem(x + d, nx)
-        rows = pl.ds(pl.multiple_of(xx * xcols, xcols), xcols)
-        return remote(
-            part.at[i, rows], rx.at[i, d], x_s.at[i, d], x_r.at[i, d], at(y, xx, c)
-        )
-
-    def z_copy(i, e):
-        zz = block_of(i, a)
-        cc = core_off(e)
-        rows = pl.ds(pl.multiple_of(cc * ccols, ccols), ccols)
-        slot = lax.rem(zz - z + nz, nz)
-        return remote(
-            xsum.at[i, rows], rz.at[slot], z_s.at[i, e], z_r.at[slot],
-            (zz, ((2 * b + c) * nx + x) * 2 + cc),
-        )
-
-    def stays(i):
-        return (block_of(i, a) == z) & (c == a)
-
-    def forward(i):
-        for d in range(1, ny):
-            att_copy(i, d).wait_recv()
-            fwd_copy(i, d).start()
-
-        @pl.when(i + ahead < hc)
-        def _():
-            send_att(i + ahead)
-
-    def product(i):
-        for d in range(ny):
-            fwd_copy(i, d).wait_recv()
-        part[i] = mm(proj_t[...], att[i], NN).astype(BF16)
-        for d in range(1, nx):
-            x_copy(i, d).start()
-
-    def add_x(i):
-        mine = pl.ds(pl.multiple_of(x * xcols, xcols), xcols)
-        total = part[i, mine].astype(F32)
-        for d in range(1, nx):
-            x_copy(i, d).wait_recv()
-            total = total + rx[i, d].astype(F32)
-        xsum[i] = total.astype(BF16)
-        here = stays(i)
-
-        @pl.when(here)
-        def _():
-            rz[0] = xsum[i, pl.ds(pl.multiple_of(c * ccols, ccols), ccols)]
-
-        @pl.when(~here)
-        def _():
-            z_copy(i, 0).start()
-
-        z_copy(i, 1).start()
-
-    def step(i, carry):
-        @pl.when(i < hc)
-        def _():
-            forward(i)
-
-        @pl.when(i > 0)
-        def _():
-            product(i - 1)
-
+    if not early:
+        turn_all()
+    for i in range(early, hc):
+        product(i)
+    for i in range(hc):
+        total = (part[i, :, x] if i % 2 == 0 else part[i, y]).astype(F32)
+        for d in range(1, nx if i % 2 == 0 else ny):
+            first_copy(i, d).wait_recv()
+            total = total + rx1[i, d].astype(F32)
+        sum1[i] = total.astype(BF16)
+        for d in range(1, ny if i % 2 == 0 else nx):
+            second_copy(i, d).start()
+    for i in range(hc):
+        total = sum1[i, y if i % 2 == 0 else x].astype(F32)
+        for d in range(1, ny if i % 2 == 0 else nx):
+            second_copy(i, d).wait_recv()
+            total = total + rx2[i, d].astype(F32)
+        sum2[i] = total.astype(BF16)
+        if i == 0:
+
+            @pl.when(stays)
+            def _():
+                rz[0] = sum2[0]
+
+            @pl.when(~stays)
+            def _():
+                z_copy(0).start()
+
+        else:
+            z_copy(i).start()
+
+    def send_far(i, carry):
+        for half in range(2):
+            start_far(i, half)
         return carry
 
-    lax.fori_loop(0, hc + 1, step, 0)
-
-    def sums(i, carry):
-        add_x(i)
-        return carry
-
-    lax.fori_loop(0, hc, sums, 0)
-
-    def late_far(i, carry):
-        for half in range(2):
-            start_far(i, half, True)
-        return carry
-
-    lax.fori_loop(0, hc, late_far, 0)
-
-    def rz_copy(slot):
-        return remote(rz.at[slot], rz.at[slot], z_s.at[0, 1], z_r.at[slot], right)
-
-    @pl.when(~((zhalf == a) & (c == a)))
+    lax.fori_loop(0, hc, send_far, 0)
+
+    @pl.when(~stays)
     def _():
-        rz_copy(0).wait_recv()
+        z_copy(0).wait_recv()
 
     grad = rz[0].astype(F32)
-    for slot in range(1, nz):
-        rz_copy(slot).wait_recv()
-        grad = grad + rz[slot].astype(F32)
+    for i in range(1, hc):
+        z_copy(i).wait_recv()
+        grad = grad + rz[i].astype(F32)
 
     piece = HEAD_DIM // chips
     for h in range(2):
@@ -477,23 +468,25 @@
                 for way in range(2):
                     halo_copy(i, half, kv, way).wait_send()
                     far_copy(i, half, kv, way).wait_send()
-        for d in range(ny):
-            if d > 0:
-                att_copy(i, d).wait_send()
-            fwd_copy(i, d).wait_send()
-        for d in range(1, nx):
-            x_copy(i, d).wait_send()
-
-        @pl.when(~stays(i))
-        def _():
-            z_copy(i, 0).wait_send()
-
-        z_copy(i, 1).wait_send()
+        for slot in range(1, 4):
+            att_copy(i, slot).wait_send()
         return carry
 
     lax.fori_loop(0, hc, drain, 0)
-    for d, e in others:
-        proj_copy(d, e).wait_send()
+    for slot in range(1, 4):
+        proj_copy(slot).wait_send()
+    for i in range(hc):
+        for d in range(1, nx if i % 2 == 0 else ny):
+            first_copy(i, d).wait_send()
+        for d in range(1, ny if i % 2 == 0 else nx):
+            second_copy(i, d).wait_send()
+        if i > 0:
+            z_copy(i).wait_send()
+
+    @pl.when(~stays)
+    def _():
+        z_copy(0).wait_send()
+
     pair.wait_send()
     swap.wait_send()
     for r in range(1, chips):
@@ -541,10 +534,9 @@
     hc = nz // 2
     tile, width = query_tiles.shape[2:]
     depth = proj_grad.shape[3]
-    qcols = depth // ny
-    xcols = qcols // nx
+    hcols = depth // 2
+    ccols = depth // seq
     cb = 2 * HEAD_DIM
-    group = ny * 2
     anyspec = pl.BlockSpec(memory_space=pl.ANY)
     chips = seq // 2
     rows = jax.ShapeDtypeStruct((tile, width), BF16)
@@ -564,13 +556,15 @@
             pltpu.VMEM(halves + (tile, cb), BF16),
             pltpu.VMEM((tile, width), F32),
             pltpu.VMEM((tile, width), F32),
-            pltpu.VMEM((group, tile, qcols), BF16),
-            pltpu.VMEM((qcols, group * tile), BF16),
-            pltpu.VMEM((hc, group * tile, cb), BF16),
-            pltpu.VMEM((hc, qcols, cb), BF16),
-            pltpu.VMEM((hc, nx, xcols, cb), BF16),
-            pltpu.VMEM((hc, xcols, cb), BF16),
-            pltpu.VMEM((nz, xcols // 2, cb), BF16),
+            pltpu.VMEM((4, tile, hcols), BF16),
+            pltpu.VMEM((hcols, 4 * tile), BF16),
+            pltpu.VMEM((hc, 4 * tile, cb), BF16),
+            pltpu.VMEM((hc, ny, nx, ccols, cb), BF16),
+            pltpu.VMEM((hc, ny, ny, ccols, cb), BF16),
+            pltpu.VMEM((hc, ny, ccols, cb), BF16),
+            pltpu.VMEM((hc, ny, ccols, cb), BF16),
+            pltpu.VMEM((hc, ccols, cb), BF16),
+            pltpu.VMEM((hc, ccols, cb), BF16),
             pltpu.VMEM((2,) + square, F32),
             pltpu.VMEM(square, F32),
             pltpu.VMEM(square, F32),
@@ -579,9 +573,10 @@
             pltpu.VMEM((2,) + square, F32),
             dma((5,)), dma((4,)),
             dma(halves), dma(halves), dma(halves), dma(halves),
-            dma((group,)), dma((group,)),
+            dma((4,)), dma((4,)),
+            dma((hc, 4)), dma((hc, 4)),
             dma((hc, ny)), dma((hc, ny)), dma((hc, ny)), dma((hc, ny)),
-            dma((hc, nx)), dma((hc, nx)), dma((hc, 2)), dma((nz,)),
+            dma((hc,)), dma((hc,)),
             dma((2,)), dma((2,)),
             dma((chips,)), dma((chips,)), dma((chips,)), dma((chips,)),
         ],

time: 96.9 us -> 86.2 us (0.89)
  Pallas kernels: 95.7 us -> 85.4 us
    pallas_call x1, Pallas kernels: 93.5 us -> 83.2 us  [local(): pl.pallas_call(functools.partial(kernel, geo), out_shape=(rows, rows, row...]
where the time goes in v3:
time: 86.2 us; the launch traced here: 86.1 us
  Pallas kernels  85.4 us (99%)
    pallas_call x1, Pallas kernels, local(): pl.pallas_call(functools.partial(kernel, geo), out_shape=(rows, rows, row...  83.2 us
    pallas_call x1, Pallas kernels, settle(): pl.pallas_call(settle_kernel, out_shape=tuple((jax.ShapeDtypeStruct(a.sha...  2.27 us

profile of v3, /device:TPU:1, one launch (start us, length us, event | category | flops | bytes accessed | tf_op | source)
XLA Modules:
  0.0 86.1 jit_solution(4603411360785305764)
XLA Ops:
  0.6 83.2 %shard_map.93 = (bf16[128,2048]{1,0:T(8,128)(2,1)}, bf16[128,2048]{1,0:T(8,128)(2,1)}, bf16[128,2048]{1,0:T(8,128)(2,1)}, f32[96,256]{1,0:T(8,128)}) custom-call(s32[1,32]{1,0:T(1,128)} %nb.1, bf16[128,2048]{1,0:T(8,128)(2,1)} %bitcast.10, bf16[128,2048]{1,0:T(8,128)(2,1)} %bitcast.11, bf16[128,2048]{1,0:T(8,128)(2,1)} %bitcast.12, ...), custom_call_target="tpu_custom_call" | custom-call | tf_op jit(solution)/shard_map/pallas_call | solution.py:546
  83.8 2.3 %shard_map.94 = (bf16[128,2048]{1,0:T(8,128)(2,1)}, bf16[128,2048]{1,0:T(8,128)(2,1)}, bf16[128,2048]{1,0:T(8,128)(2,1)}, f32[96,256]{1,0:T(8,128)}) custom-call(bf16[128,2048]{1,0:T(8,128)(2,1)} %get-tuple-element.12.refs_0_, bf16[128,2048]{1,0:T(8,128)(2,1)} %get-tuple-element.13.refs_1_, bf16[128,2048]{1,0:T(8,128)(2,1)} %get-tuple-element.14.refs_2_, ...), custom_call_target="tpu_custom_call" | custom-call | tf_op jit(solution)/shard_map/pallas_call | solution.py:521

commit v4 on v3

--- a/solution.py
+++ b/solution.py
@@ -53,17 +53,17 @@
     geo,
     nb,
     q_hbm, k_hbm, v_hbm, do_hbm, proj_hbm,
-    dq_hbm, dk_hbm, dv_hbm, upd_hbm,
+    dq_v, dk_v, dv_v, upd_v,
     q_v, k_v, v_v, do_v,
-    dq_v, dk_v, dv_v, upd_v,
     halo, far_out, far_in, own_k, own_v,
     proj_all, proj_t, att, part, rx1, sum1, rx2, sum2, rz,
     g_part, g_pair, g_mine, g_in, g_full, poly_all,
-    in_sem, out_sem,
+    in_sem,
     halo_s, halo_r, far_s, far_r,
     proj_s, proj_r,
     att_s, att_r, s1_s, s1_r, s2_s, s2_r, z_s, z_r,
     pair_s, pair_r, g1_s, g1_r, g2_s, g2_r,
+    from_below, from_above, from_far,
 ):
     nz, ny, nx = geo
     seq = ny * nx * 2
@@ -135,26 +135,15 @@
 
     stays = (c == p) & (p * ys + y // 2 == y) & (lax.rem(y, 2) == c)
 
-    for r in range(1, chips):
-        greet((z, chip_off(r) * 2 + c))
-    greet(other_core)
-    greet(mate(c))
-    greet(mate(1 - c))
-    greet(right)
-    greet(left)
-    source_chip = (2 * lax.rem(y, ys) + c) * nx + x
-    for m in range(1, hc):
-        greet(owner(m))
-        greet((2 * lax.rem(zp + m, hc) + y // ys, source_chip * 2 + p))
-
-    @pl.when(~stays)
-    def _():
-        greet(owner(0))
-        greet((2 * zp + y // ys, source_chip * 2 + p))
-
-    pl.semaphore_wait(
-        barrier, chips - 1 + 5 + 2 * (hc - 1) + jnp.where(stays, 0, 2)
-    )
+    above = (lax.rem(z + 2, nz), s)
+    below = (lax.rem(z + nz - 2, nz), s)
+    for d in range(1, nx):
+        greet(at(y, lax.rem(x + d, nx), c))
+    for d in range(1, ny):
+        greet(at(y_off(d), x, c))
+    for dev in (other_core, mate(c), mate(1 - c), right, left, above, below):
+        greet(dev)
+    pl.semaphore_wait(barrier, nx + ny - 2 + 7)
 
     def halo_copy(i, half, kv, way):
         t = 2 * i + half
@@ -260,6 +249,7 @@
             first_copy(i, d).start()
 
     early = min(2, hc - 1)
+    far_early = min(1, hc - 1)
 
     def attend(i, carry):
         if early:
@@ -309,6 +299,12 @@
                 att_copy(i, 3).start()
                 att_copy(i, 1).start()
 
+            if far_early:
+
+                @pl.when(i < far_early)
+                def _():
+                    start_far(i, half)
+
         @pl.when(i == max(hc - 2, 0))
         def _():
             proj_copy(2).wait_recv()
@@ -317,13 +313,20 @@
         return carry
 
     lax.fori_loop(0, hc, attend, 0)
-    dq_out = pltpu.make_async_copy(dq_v, dq_hbm, out_sem.at[0])
-    dq_out.start()
 
     if not early:
         turn_all()
     for i in range(early, hc):
         product(i)
+
+    def tell(sem, dev):
+        pl.semaphore_signal(sem, inc=1, device_id=dev, device_id_type=MESH)
+
+    tell(from_below, above)
+    tell(from_above, below)
+    pl.semaphore_wait(from_below, 1)
+    pl.semaphore_wait(from_above, 1)
+    tell(from_far, above)
     for i in range(hc):
         total = (part[i, :, x] if i % 2 == 0 else part[i, y]).astype(F32)
         for d in range(1, nx if i % 2 == 0 else ny):
@@ -339,6 +342,7 @@
             total = total + rx2[i, d].astype(F32)
         sum2[i] = total.astype(BF16)
         if i == 0:
+            pl.semaphore_wait(from_far, 1)
 
             @pl.when(stays)
             def _():
@@ -356,7 +360,7 @@
             start_far(i, half)
         return carry
 
-    lax.fori_loop(0, hc, send_far, 0)
+    lax.fori_loop(far_early, hc, send_far, 0)
 
     @pl.when(~stays)
     def _():
@@ -426,11 +430,6 @@
         return carry
 
     lax.fori_loop(0, hc, gather_far, 0)
-    dk_out = pltpu.make_async_copy(dk_v, dk_hbm, out_sem.at[1])
-    dv_out = pltpu.make_async_copy(dv_v, dv_hbm, out_sem.at[2])
-    dk_out.start()
-    dv_out.start()
-
     for r in range(1, chips):
         g2_from(r).wait_recv()
 
@@ -459,9 +458,6 @@
         part_h = grad[:, h * HEAD_DIM : (h + 1) * HEAD_DIM]
         result = mmh(part_h, poly_all[h], NT)
         upd_v[:, h * HEAD_DIM : (h + 1) * HEAD_DIM] = result * (0.2 * D**0.5)
-    upd_out = pltpu.make_async_copy(upd_v, upd_hbm, out_sem.at[3])
-    upd_out.start()
-
     def drain(i, carry):
         for half in range(2):
             for kv in range(2):
@@ -492,24 +488,15 @@
     for r in range(1, chips):
         g1_copy(r).wait_send()
         g2_copy(r).wait_send()
-    for out in (dq_out, dk_out, dv_out, upd_out):
-        out.wait()
 
 
 def settle_kernel(*refs):
-    count = (len(refs) - 2) // 3
-    ins, outs, kept = refs[:count], refs[count : 2 * count], refs[2 * count : 3 * count]
-    in_sem, out_sem = refs[-2:]
-    loads = [
-        pltpu.make_async_copy(ins[n], kept[n], in_sem.at[n]) for n in range(count)
+    count = len(refs) // 2
+    sem = refs[-1]
+    stores = [
+        pltpu.make_async_copy(refs[n], refs[count + n], sem.at[n]) for n in range(count)
     ]
-    stores = [
-        pltpu.make_async_copy(kept[n], outs[n], out_sem.at[n]) for n in range(count)
-    ]
-    for load in loads:
-        load.start()
-    for load, store in zip(loads, stores):
-        load.wait()
+    for store in stores:
         store.start()
     for store in stores:
         store.wait()
@@ -523,8 +510,8 @@
         out_shape=tuple(jax.ShapeDtypeStruct(a.shape, a.dtype) for a in arrays),
         in_specs=[anyspec] * len(arrays),
         out_specs=(anyspec,) * len(arrays),
-        scratch_shapes=[pltpu.VMEM(a.shape, a.dtype) for a in arrays] + [sems, sems],
-        compiler_params=pltpu.CompilerParams(vmem_limit_bytes=60 * 2**20),
+        scratch_shapes=[sems],
+        compiler_params=pltpu.CompilerParams(vmem_limit_bytes=8 * 2**20),
     )(*arrays)
 
 
@@ -539,18 +526,17 @@
     cb = 2 * HEAD_DIM
     anyspec = pl.BlockSpec(memory_space=pl.ANY)
     chips = seq // 2
-    rows = jax.ShapeDtypeStruct((tile, width), BF16)
+    rows = pltpu.VMEM((tile, width), BF16)
     dma = pltpu.SemaphoreType.DMA
     halves = (2, 2, 2 * hc)
     square = (HEAD_DIM, HEAD_DIM)
     out = pl.pallas_call(
         functools.partial(kernel, geo),
-        out_shape=(rows, rows, rows, jax.ShapeDtypeStruct((depth // seq, cb), F32)),
+        out_shape=(rows, rows, rows, pltpu.VMEM((depth // seq, cb), F32)),
         in_specs=[pl.BlockSpec(memory_space=pltpu.SMEM)] + [anyspec] * 5,
-        out_specs=(anyspec,) * 4,
-        scratch_shapes=[pltpu.VMEM((tile, width), BF16)] * 7
+        out_specs=(pl.BlockSpec(memory_space=pltpu.VMEM),) * 4,
+        scratch_shapes=[pltpu.VMEM((tile, width), BF16)] * 4
         + [
-            pltpu.VMEM((depth // seq, cb), F32),
             pltpu.VMEM(halves + (tile, cb), BF16),
             pltpu.VMEM((3, 2 * hc, tile, cb), BF16),
             pltpu.VMEM(halves + (tile, cb), BF16),
@@ -571,7 +557,7 @@
             pltpu.VMEM((chips, HEAD_DIM // chips, HEAD_DIM), F32),
             pltpu.VMEM(square, F32),
             pltpu.VMEM((2,) + square, F32),
-            dma((5,)), dma((4,)),
+            dma((5,)),
             dma(halves), dma(halves), dma(halves), dma(halves),
             dma((4,)), dma((4,)),
             dma((hc, 4)), dma((hc, 4)),
@@ -579,9 +565,11 @@
             dma((hc,)), dma((hc,)),
             dma((2,)), dma((2,)),
             dma((chips,)), dma((chips,)), dma((chips,)), dma((chips,)),
+            pltpu.SemaphoreType.REGULAR, pltpu.SemaphoreType.REGULAR,
+            pltpu.SemaphoreType.REGULAR,
         ],
         compiler_params=pltpu.CompilerParams(
-            collective_id=0, has_side_effects=True, vmem_limit_bytes=60 * 2**20
+            collective_id=0, has_side_effects=True, vmem_limit_bytes=62 * 2**20
         ),
     )(
         neighbour, query_tiles[0, 0], key_tiles[0, 0], value_tiles[0, 0],

time: 86.2 us -> 80.4 us (0.933)
  Pallas kernels: 85.4 us -> 79.6 us
    pallas_call x1, Pallas kernels: 83.2 us -> 78.4 us  [local(): pl.pallas_call(functools.partial(kernel, geo), out_shape=(rows, rows, row...]
    pallas_call x1, Pallas kernels: 2.27 us -> 1.2 us  [settle(): pl.pallas_call(settle_kernel, out_shape=tuple((jax.ShapeDtypeStruct(a.sha...]
where the time goes in v4:
time: 80.4 us; the launch traced here: 80.3 us
  Pallas kernels  79.6 us (99%)
    pallas_call x1, Pallas kernels, local(): pl.pallas_call(functools.partial(kernel, geo), out_shape=(rows, rows, row...  78.4 us

profile of v4, /device:TPU:1, one launch (start us, length us, event | category | flops | bytes accessed | tf_op | source)
XLA Modules:
  0.0 80.3 jit_solution(10603902753812351856)
XLA Ops:
  0.6 78.4 %shard_map.93 = (bf16[128,2048]{1,0:T(8,128)(2,1)S(1)}, bf16[128,2048]{1,0:T(8,128)(2,1)S(1)}, bf16[128,2048]{1,0:T(8,128)(2,1)S(1)}, f32[96,256]{1,0:T(8,128)S(1)}) custom-call(s32[1,32]{1,0:T(1,128)} %nb.1, bf16[128,2048]{1,0:T(8,128)(2,1)} %bitcast.10, bf16[128,2048]{1,0:T(8,128)(2,1)} %bitcast.11, bf16[128,2048]{1,0:T(8,128)(2,1)} %bitcast.12, ...), custom_call_target="tpu_custom_call" | custom-call | tf_op jit(solution)/shard_map/pallas_call | solution.py:533
  79.1 1.2 %shard_map.94 = (bf16[128,2048]{1,0:T(8,128)(2,1)}, bf16[128,2048]{1,0:T(8,128)(2,1)}, bf16[128,2048]{1,0:T(8,128)(2,1)}, f32[96,256]{1,0:T(8,128)}) custom-call(bf16[128,2048]{1,0:T(8,128)(2,1)S(1)} %get-tuple-element.12.refs_0_, bf16[128,2048]{1,0:T(8,128)(2,1)S(1)} %get-tuple-element.13.refs_1_, bf16[128,2048]{1,0:T(8,128)(2,1)S(1)} %get-tuple-element.14.refs_2_, ...), custom_call_target="tpu_custom_call" | custom-call | tf_op jit(solution)/shard_map/pallas_call | solution.py:508

commit v5 on v4

--- a/solution.py
+++ b/solution.py
@@ -32,21 +32,32 @@
     return lax.dot_general(a, b, dims, precision=BEST, preferred_element_type=F32)
 
 
-def head_grads(q, kk, vv, do):
+def head_grads(heads):
     score_scale = HEAD_DIM ** (-0.5)
-    scores = mm(q, kk, NT) * score_scale
-    row_max = jnp.max(scores, axis=1, keepdims=True)
-    exp_scores = jnp.exp(scores - row_max)
-    weights = exp_scores / jnp.sum(exp_scores, axis=1, keepdims=True)
-    weights_b = weights.astype(BF16)
-    attended = mm(weights_b, vv, NN).astype(BF16)
-    delta = jnp.sum(do.astype(F32) * attended.astype(F32), axis=1, keepdims=True)
-    dweights = mm(do, vv, NT)
-    dscore_b = (weights * (dweights - delta)).astype(BF16)
-    dq = (mm(dscore_b, kk, NN) * score_scale).astype(BF16)
-    dk = mm(dscore_b, q, TN) * score_scale
-    dv = mm(weights_b, do, TN)
-    return dq, dk, dv, attended
+    scores = [mm(q, kk, NT) for q, kk, vv, do in heads]
+    dweights = [mm(do, vv, NT) for q, kk, vv, do in heads]
+    row_max = [jnp.max(t, axis=1, keepdims=True) for t in scores]
+    exp_scores = [jnp.exp((t - m) * score_scale) for t, m in zip(scores, row_max)]
+    inverse = [1.0 / jnp.sum(t, axis=1, keepdims=True) for t in exp_scores]
+    weights = [t * r for t, r in zip(exp_scores, inverse)]
+    weights_b = [t.astype(BF16) for t in weights]
+    attended = [
+        mm(t, vv, NN).astype(BF16) for t, (q, kk, vv, do) in zip(weights_b, heads)
+    ]
+    delta = [
+        jnp.sum(do.astype(F32) * t.astype(F32), axis=1, keepdims=True)
+        for t, (q, kk, vv, do) in zip(attended, heads)
+    ]
+    dv = [mm(t, do, TN) for t, (q, kk, vv, do) in zip(weights_b, heads)]
+    dscore_b = [
+        (w * (dw - dl)).astype(BF16) for w, dw, dl in zip(weights, dweights, delta)
+    ]
+    dq = [
+        (mm(t, kk, NN) * score_scale).astype(BF16)
+        for t, (q, kk, vv, do) in zip(dscore_b, heads)
+    ]
+    dk = [mm(t, q, TN) * score_scale for t, (q, kk, vv, do) in zip(dscore_b, heads)]
+    return list(zip(dq, dk, dv, attended))
 
 
 def kernel(
@@ -145,23 +156,6 @@
         greet(dev)
     pl.semaphore_wait(barrier, nx + ny - 2 + 7)
 
-    def halo_copy(i, half, kv, way):
-        t = 2 * i + half
-        src = (k_hbm, v_hbm)[kv].at[:, lanes(block_of(i, half))]
-        return remote(
-            src, halo.at[way, kv, t], halo_s.at[way, kv, t], halo_r.at[way, kv, t],
-            (right, left)[way],
-        )
-
-    def start_halo(i, carry):
-        for half in range(2):
-            for kv in range(2):
-                for way in range(2):
-                    halo_copy(i, half, kv, way).start()
-        return carry
-
-    lax.fori_loop(0, hc, start_halo, 0)
-
     def proj_copy(slot):
         if slot == 3:
             src = proj_all.at[2]
@@ -174,6 +168,23 @@
 
     proj_copy(2).start()
     proj_copy(1).start()
+    def halo_copy(i, half, kv, way):
+        t = 2 * i + half
+        src = (k_hbm, v_hbm)[kv].at[:, lanes(block_of(i, half))]
+        return remote(
+            src, halo.at[way, kv, t], halo_s.at[way, kv, t], halo_r.at[way, kv, t],
+            (right, left)[way],
+        )
+
+    def start_halo(i, carry):
+        for half in range(2):
+            for kv in range(2):
+                for way in range(2):
+                    halo_copy(i, half, kv, way).start()
+        return carry
+
+    lax.fori_loop(0, hc, start_halo, 0)
+
     for load in loads:
         load.wait()
 
@@ -216,11 +227,9 @@
                 ]
 
     def turn_all():
-        turn(0)
         turn(2)
-        for slot in (1, 3):
-            proj_copy(slot).wait_recv()
-            turn(slot)
+        proj_copy(3).wait_recv()
+        turn(3)
 
     def first_copy(i, d):
         if i % 2 == 0:
@@ -261,33 +270,42 @@
                     product(k)
 
         for half in range(2):
-            t = 2 * i + half
-            block = block_of(i, half)
             for kv in range(2):
                 for way in range(2):
                     halo_copy(i, half, kv, way).wait_recv()
-            for h in range(2):
-                inside = pl.ds(h * HEAD_DIM, HEAD_DIM)
-                cols = pl.ds(
-                    pl.multiple_of(block * cb + h * HEAD_DIM, HEAD_DIM), HEAD_DIM
-                )
-
-                def beside(kv):
-                    from_left = halo[0, kv, t, :, inside].astype(F32) * go_left
-                    from_right = halo[1, kv, t, :, inside].astype(F32) * go_right
-                    return (from_left + from_right).astype(BF16)
-
-                q = q_v[:, cols]
-                do = do_v[:, cols]
-                kk = jnp.concatenate([k_v[:, cols], beside(0)], 0)
-                vv = jnp.concatenate([v_v[:, cols], beside(1)], 0)
-                dq, dk, dv, attended = head_grads(q, kk, vv, do)
-                dq_v[:, cols] = dq
-                own_k[:, cols] = dk[:tile]
-                own_v[:, cols] = dv[:tile]
-                far_out[0, t, :, inside] = dk[tile:].astype(BF16)
-                far_out[1, t, :, inside] = dv[tile:].astype(BF16)
-                far_out[2, t, :, inside] = attended
+
+        def place(half, h):
+            start = block_of(i, half) * cb + h * HEAD_DIM
+            return pl.ds(pl.multiple_of(start, HEAD_DIM), HEAD_DIM)
+
+        def beside(kv, half, h):
+            t = 2 * i + half
+            inside = pl.ds(h * HEAD_DIM, HEAD_DIM)
+            from_left = halo[0, kv, t, :, inside].astype(F32) * go_left
+            from_right = halo[1, kv, t, :, inside].astype(F32) * go_right
+            return (from_left + from_right).astype(BF16)
+
+        names = [(half, h) for half in range(2) for h in range(2)]
+        heads = [
+            (
+                q_v[:, place(*n)],
+                jnp.concatenate([k_v[:, place(*n)], beside(0, *n)], 0),
+                jnp.concatenate([v_v[:, place(*n)], beside(1, *n)], 0),
+                do_v[:, place(*n)],
+            )
+            for n in names
+        ]
+        for n, (dq, dk, dv, attended) in zip(names, head_grads(heads)):
+            t = 2 * i + n[0]
+            inside = pl.ds(n[1] * HEAD_DIM, HEAD_DIM)
+            far_out[2, t, :, inside] = attended
+            dq_v[:, place(*n)] = dq
+            own_k[:, place(*n)] = dk[:tile]
+            own_v[:, place(*n)] = dv[:tile]
+            far_out[0, t, :, inside] = dk[tile:].astype(BF16)
+            far_out[1, t, :, inside] = dv[tile:].astype(BF16)
+        for half in range(2):
+            t = 2 * i + half
 
             @pl.when(c == half)
             def _():
@@ -312,6 +330,9 @@
 
         return carry
 
+    turn(0)
+    proj_copy(1).wait_recv()
+    turn(1)
     lax.fori_loop(0, hc, attend, 0)
 
     if not early:
@@ -355,13 +376,6 @@
         else:
             z_copy(i).start()
 
-    def send_far(i, carry):
-        for half in range(2):
-            start_far(i, half)
-        return carry
-
-    lax.fori_loop(far_early, hc, send_far, 0)
-
     @pl.when(~stays)
     def _():
         z_copy(0).wait_recv()
@@ -414,22 +428,13 @@
     for r in range(1, chips):
         g2_copy(r).start()
 
-    def gather_far(i, carry):
+    def send_far(i, carry):
         for half in range(2):
-            t = 2 * i + half
-            cols = lanes(block_of(i, half))
-            for kv in range(2):
-                for way in range(2):
-                    far_copy(i, half, kv, way).wait_recv()
-                out = (dk_v, dv_v)[kv]
-                out[:, cols] = (
-                    (own_k, own_v)[kv][:, cols]
-                    + far_in[0, kv, t].astype(F32) * left_sends
-                    + far_in[1, kv, t].astype(F32) * right_sends
-                ).astype(BF16)
+            start_far(i, half)
         return carry
 
-    lax.fori_loop(0, hc, gather_far, 0)
+    lax.fori_loop(far_early, hc, send_far, 0)
+
     for r in range(1, chips):
         g2_from(r).wait_recv()
 
@@ -458,6 +463,22 @@
         part_h = grad[:, h * HEAD_DIM : (h + 1) * HEAD_DIM]
         result = mmh(part_h, poly_all[h], NT)
         upd_v[:, h * HEAD_DIM : (h + 1) * HEAD_DIM] = result * (0.2 * D**0.5)
+    def gather_far(i, carry):
+        for half in range(2):
+            t = 2 * i + half
+            cols = lanes(block_of(i, half))
+            for kv in range(2):
+                for way in range(2):
+                    far_copy(i, half, kv, way).wait_recv()
+                out = (dk_v, dv_v)[kv]
+                out[:, cols] = (
+                    (own_k, own_v)[kv][:, cols]
+                    + far_in[0, kv, t].astype(F32) * left_sends
+                    + far_in[1, kv, t].astype(F32) * right_sends
+                ).astype(BF16)
+        return carry
+
+    lax.fori_loop(0, hc, gather_far, 0)
     def drain(i, carry):
         for half in range(2):
             for kv in range(2):

time: 80.4 us -> 79.6 us (0.990)
  no operation moved by 1% of the time
where the time goes in v5:
time: 79.6 us; the launch traced here: 79.5 us
  Pallas kernels  78.8 us (99%)
    pallas_call x1, Pallas kernels, local(): pl.pallas_call(functools.partial(kernel, geo), out_shape=(rows, rows, row...  77.6 us

profile of v5, /device:TPU:1, one launch (start us, length us, event | category | flops | bytes accessed | tf_op | source)
XLA Modules:
  0.0 79.5 jit_solution(1259537819395101913)
XLA Ops:
  0.6 77.6 %shard_map.93 = (bf16[128,2048]{1,0:T(8,128)(2,1)S(1)}, bf16[128,2048]{1,0:T(8,128)(2,1)S(1)}, bf16[128,2048]{1,0:T(8,128)(2,1)S(1)}, f32[96,256]{1,0:T(8,128)S(1)}) custom-call(s32[1,32]{1,0:T(1,128)} %nb.1, bf16[128,2048]{1,0:T(8,128)(2,1)} %bitcast.10, bf16[128,2048]{1,0:T(8,128)(2,1)} %bitcast.11, bf16[128,2048]{1,0:T(8,128)(2,1)} %bitcast.12, ...), custom_call_target="tpu_custom_call" | custom-call | tf_op jit(solution)/shard_map/pallas_call | solution.py:554
  78.3 1.2 %shard_map.94 = (bf16[128,2048]{1,0:T(8,128)(2,1)}, bf16[128,2048]{1,0:T(8,128)(2,1)}, bf16[128,2048]{1,0:T(8,128)(2,1)}, f32[96,256]{1,0:T(8,128)}) custom-call(bf16[128,2048]{1,0:T(8,128)(2,1)S(1)} %get-tuple-element.12.refs_0_, bf16[128,2048]{1,0:T(8,128)(2,1)S(1)} %get-tuple-element.13.refs_1_, bf16[128,2048]{1,0:T(8,128)(2,1)S(1)} %get-tuple-element.14.refs_2_, ...), custom_call_target="tpu_custom_call" | custom-call | tf_op jit(solution)/shard_map/pallas_call | solution.py:529

commit v6 on v5

--- a/solution.py
+++ b/solution.py
@@ -386,15 +386,17 @@
         grad = grad + rz[i].astype(F32)
 
     piece = HEAD_DIM // chips
-    for h in range(2):
-        part_h = grad[:, h * HEAD_DIM : (h + 1) * HEAD_DIM]
-        g_part[h] = mmh(part_h, part_h, TN)
+    first, second = grad[:, :HEAD_DIM], grad[:, HEAD_DIM:]
+    mine = jnp.where(c == 0, first, second)
+    theirs = jnp.where(c == 0, second, first)
+    g_part[1 - c] = mmh(theirs, theirs, TN)
     pair = remote(
         g_part.at[1 - c], g_pair, pair_s.at[0], pair_r.at[0], other_core
     )
     pair.start()
+    own_gram = mmh(mine, mine, TN)
     pair.wait_recv()
-    g_mine[...] = g_part[c] + g_pair[...]
+    g_mine[...] = own_gram + g_pair[...]
 
     def rows_of(index):
         return pl.ds(pl.multiple_of(index * piece, piece), piece)
@@ -456,13 +458,18 @@
         poly_all.at[c], poly_all.at[c], pair_s.at[1], pair_r.at[1], other_core
     )
     swap.start()
+
+    def finish(head, part_h):
+        result = mmh(part_h, poly_all[head], NT)
+        place_h = pl.ds(pl.multiple_of(head * HEAD_DIM, HEAD_DIM), HEAD_DIM)
+        upd_v[:, place_h] = result * (0.2 * D**0.5)
+
+    finish(c, mine)
     remote(
         poly_all.at[1 - c], poly_all.at[1 - c], pair_s.at[1], pair_r.at[1], other_core
     ).wait_recv()
-    for h in range(2):
-        part_h = grad[:, h * HEAD_DIM : (h + 1) * HEAD_DIM]
-        result = mmh(part_h, poly_all[h], NT)
-        upd_v[:, h * HEAD_DIM : (h + 1) * HEAD_DIM] = result * (0.2 * D**0.5)
+    finish(1 - c, theirs)
+
     def gather_far(i, carry):
         for half in range(2):
             t = 2 * i + half

time: 79.6 us -> 79.9 us (level)
  no operation moved by 1% of the time
where the time goes in v6:
time: 79.9 us; the launch traced here: 79.8 us
  Pallas kernels  79.1 us (99%)
    pallas_call x1, Pallas kernels, local(): pl.pallas_call(functools.partial(kernel, geo), out_shape=(rows, rows, row...  77.9 us

profile of v6, /device:TPU:1, one launch (start us, length us, event | category | flops | bytes accessed | tf_op | source)
XLA Modules:
  0.0 79.8 jit_solution(14364274127790080397)
XLA Ops:
  0.6 77.9 %shard_map.93 = (bf16[128,2048]{1,0:T(8,128)(2,1)S(1)}, bf16[128,2048]{1,0:T(8,128)(2,1)S(1)}, bf16[128,2048]{1,0:T(8,128)(2,1)S(1)}, f32[96,256]{1,0:T(8,128)S(1)}) custom-call(s32[1,32]{1,0:T(1,128)} %nb.1, bf16[128,2048]{1,0:T(8,128)(2,1)} %bitcast.10, bf16[128,2048]{1,0:T(8,128)(2,1)} %bitcast.11, bf16[128,2048]{1,0:T(8,128)(2,1)} %bitcast.12, ...), custom_call_target="tpu_custom_call" | custom-call | tf_op jit(solution)/shard_map/pallas_call | solution.py:561
  78.6 1.2 %shard_map.94 = (bf16[128,2048]{1,0:T(8,128)(2,1)}, bf16[128,2048]{1,0:T(8,128)(2,1)}, bf16[128,2048]{1,0:T(8,128)(2,1)}, f32[96,256]{1,0:T(8,128)}) custom-call(bf16[128,2048]{1,0:T(8,128)(2,1)S(1)} %get-tuple-element.12.refs_0_, bf16[128,2048]{1,0:T(8,128)(2,1)S(1)} %get-tuple-element.13.refs_1_, bf16[128,2048]{1,0:T(8,128)(2,1)S(1)} %get-tuple-element.14.refs_2_, ...), custom_call_target="tpu_custom_call" | custom-call | tf_op jit(solution)/shard_map/pallas_call | solution.py:536
